TPU v7x, 32 devices: a whole 2x2x4 slice. The times are simulated.
32 devices in a mesh: group: 16 (over z, y, core), tok: 2 (over x).
Axes of the slice: x: 2, y: 2, z: 4, core: 2. Of those that a mesh axis runs over, the one named last changes fastest.
Arguments:
- latents: bfloat16 [4096, 5120], P(('group', 'tok')), may hold values from -6 to 6
- timesteps: int32 [16], P('group'), may hold values from 0 to 999
- mod_shift: float32 [5120], replicated, may hold values from -3 to 3
- mod_scale: float32 [5120], replicated, may hold values from -1.5 to 1.5
- w_query: bfloat16 [5120, 3072], P('group', 'tok'), may hold values from -7 to 7
- w_key: bfloat16 [5120, 3072], P('group', 'tok'), may hold values from -7 to 7
- w_value: bfloat16 [5120, 3072], P('group', 'tok'), may hold values from -0.078125 to 0.078125
- query_gain: float32 [3072], P('tok'), may hold values from 0.5 to 1.5
- key_gain: float32 [3072], P('tok'), may hold values from 0.5 to 1.5
- cache_keys: bfloat16 [4096, 3072], P('group', 'tok'), may hold values from -85 to 85
- cache_values: bfloat16 [4096, 3072], P('group', 'tok'), may hold values from -6 to 6
- owners: int32 [16], replicated, may hold values from 0 to 15, each once
- tile_mask: int32 [24, 2, 6], P('tok'), may hold values from 0 to 1, as said below
Outputs:
- attended: bfloat16 [4096, 3072], P('group', 'tok')
Inputs may be any that keep to these rules, and one draw needn't show every extreme that they name: `tile_mask`: each query tile i of each head sees 1 to 6 key tiles, always tile 2 * 2 + i; some query tile sees exactly 6.
All inputs are finite; a program needn't handle non-finite values.
Results may differ from a plain program's by a relative error of at most 0.012.
The roundings to bfloat16 on the way count: a program that leaves them out, or rounds other values in their place, can miss the bound.
Values may be sent and summed in bfloat16 or wider, within the bound.
A program may use at most 128 MiB of HBM per device.

v0:
```python
import math

import jax
import jax.numpy as jnp
from jax import lax
from jax.sharding import PartitionSpec as P

EPSILON = 1e-06


def from_behind(block, axis, distance):
    devices = range(lax.axis_size(axis))
    route = [(i - distance, i) for i in devices if i - distance in devices]
    return lax.ppermute(block, axis, route)


def spread_2(value, axis, source):
    kept = jnp.where(lax.axis_index(axis) == source, value, 0).astype(value.dtype)
    return lax.psum(kept, axis)


def modulate(rows_block, timestep, mod_shift, mod_scale):
    values = rows_block.astype(jnp.float32)
    width = values.shape[-1]
    centred = values - jnp.mean(values, axis=-1, keepdims=True)
    spread = jnp.mean(centred * centred, axis=-1, keepdims=True)
    normed = centred * lax.rsqrt(spread + EPSILON)
    freqs = jnp.exp(-math.log(10000.0) * jnp.arange(width, dtype=jnp.float32) / width)
    angles = timestep.astype(jnp.float32) * freqs
    return (
        normed * (1.0 + mod_scale + 0.5 * jnp.cos(angles)) + mod_shift + 0.5 * jnp.sin(angles)
    ).astype(jnp.bfloat16)


def scaled_rows(raw, squares, width, gain):
    return (raw * lax.rsqrt(squares / width + EPSILON)[:, None] * gain).astype(jnp.bfloat16)


def dense_attention(query_heads, key_heads, value_heads, allowed, tile_rows, score_scale):
    group_rows = query_heads.shape[1]
    block_rows = 512 if group_rows % 512 == 0 else group_rows
    block_count = group_rows // block_rows
    tiles_per_block = block_rows // tile_rows

    def one_head(operands):
        query_head, key_head, value_head, head_mask = operands
        key_mask = jnp.repeat(head_mask, tile_rows, axis=1)

        def one_block(block_index):
            block_queries = lax.dynamic_slice_in_dim(
                query_head, block_index * block_rows, block_rows, 0
            )
            block_mask = lax.dynamic_slice_in_dim(
                key_mask, block_index * tiles_per_block, tiles_per_block, 0
            )
            row_mask = jnp.repeat(block_mask, tile_rows, axis=0)
            scores = (
                jnp.einsum("id,jd->ij", block_queries, key_head, preferred_element_type=jnp.float32)
                * score_scale
            )
            scores = jnp.where(row_mask > 0, scores, -jnp.inf)
            peak = jnp.max(scores, axis=-1, keepdims=True)
            weights = jnp.exp(scores - peak)
            summed = jnp.dot(
                weights.astype(jnp.bfloat16), value_head, preferred_element_type=jnp.float32
            )
            return (summed / jnp.sum(weights, axis=-1, keepdims=True)).astype(jnp.bfloat16)

        blocks_out = lax.map(one_block, jnp.arange(block_count, dtype=jnp.int32))
        return blocks_out.reshape(group_rows, query_head.shape[1])

    return lax.map(one_head, (query_heads, key_heads, value_heads, allowed))


def local(
    latents,
    timesteps,
    mod_shift,
    mod_scale,
    w_query,
    w_key,
    w_value,
    query_gain,
    key_gain,
    cache_keys,
    cache_values,
    owners,
    tile_mask,
):
    modulated = modulate(latents, timesteps[0], mod_shift, mod_scale)
    root = owners[owners.shape[0] - 1]
    head_cols = w_query.shape[1]
    slabs = (
        lax.all_gather(w_query, "group", axis=0, tiled=True),
        lax.all_gather(w_key, "group", axis=0, tiled=True),
        lax.all_gather(w_value, "group", axis=0, tiled=True),
    )
    joined = jnp.concatenate(slabs, axis=1)
    projected = jnp.dot(
        lax.all_gather(modulated, "tok", axis=0, tiled=True),
        joined,
        preferred_element_type=jnp.float32,
    )
    raw_query = projected[:, :head_cols]
    raw_key = projected[:, head_cols : 2 * head_cols]
    raw_value = projected[:, 2 * head_cols :]
    query_squares, key_squares = lax.psum(
        (jnp.sum(raw_query * raw_query, axis=1), jnp.sum(raw_key * raw_key, axis=1)), "tok"
    )
    width = head_cols * lax.axis_size("tok")
    query_rows = scaled_rows(raw_query, query_squares, width, query_gain)
    key_rows = scaled_rows(raw_key, key_squares, width, key_gain)
    value_rows = raw_value.astype(jnp.bfloat16)
    earlier_keys, earlier_values = from_behind((key_rows, value_rows), "group", 1)
    cached = (spread_2(cache_keys, "group", root), spread_2(cache_values, "group", root))
    group_rows = query_rows.shape[0]
    local_heads = tile_mask.shape[0]
    query_tiles = tile_mask.shape[1]
    key_tile_count = tile_mask.shape[2]
    tile_rows = group_rows // query_tiles
    head_size = head_cols // local_heads
    score_scale = 1.0 / math.sqrt(head_size)
    context_keys = jnp.concatenate([cached[0], earlier_keys, key_rows], axis=0)
    context_values = jnp.concatenate([cached[1], earlier_values, value_rows], axis=0)
    is_first = lax.axis_index("group") == 0
    tile_ids = jnp.arange(key_tile_count, dtype=jnp.int32)
    earlier_region = (tile_ids >= query_tiles) & (tile_ids < 2 * query_tiles)
    allowed = jnp.where(earlier_region[None, None, :] & is_first, 0, tile_mask)
    query_heads = query_rows.reshape(group_rows, local_heads, head_size).transpose(1, 0, 2)
    key_heads = context_keys.reshape(3 * group_rows, local_heads, head_size).transpose(1, 0, 2)
    value_heads = context_values.reshape(3 * group_rows, local_heads, head_size).transpose(1, 0, 2)
    attended = dense_attention(query_heads, key_heads, value_heads, allowed, tile_rows, score_scale)
    return attended.transpose(1, 0, 2).reshape(group_rows, head_cols)


def solution(mesh):
    return jax.shard_map(
        local,
        mesh=mesh,
        in_specs=(
            P(("group", "tok"), None),
            P("group"),
            P(),
            P(),
            P("group", "tok"),
            P("group", "tok"),
            P("group", "tok"),
            P("tok"),
            P("tok"),
            P("group", "tok"),
            P("group", "tok"),
            P(),
            P("tok", None, None),
        ),
        out_specs=P("group", "tok"),
        check_vma=False,
    )
```

profile of v0, /device:TPU:0, one launch (start us, length us, event | category | flops | bytes accessed | tf_op | source)
XLA Modules:
  0.0 583.2 jit_solution(5719715552951323310)
XLA Ops:
  7.3 1.6 convert_reduce_fusion
  8.9 1.8 fusion.23
  10.9 1.7 fusion.27
  12.7 0.7 all-gather.11.cloned.1.call-update
  13.4 0.7 all-gather.7.cloned.1.call-update
  14.1 0.5 all-gather.9.cloned.1.call-update
  14.7 0.6 slice.14
  16.0 1.3 broadcast_select_fusion
  17.3 37.2 %all-gather.5.cloned.1.call-done = bf16[256,5120]{1,0:T(8,128)(2,1)} async-done(((bf16[128,5120]{1,0:T(8,128)(2,1)}), bf16[256,5120]{1,0:T(8,128)(2,1)}) %all-gather.5.cloned.1.call-update) | async-done | bytes 2621456 | tf_op jit(solution)/shard_map/all_gather | solution.py:100
  54.5 122.6 %all-gather.11.cloned.1.call-done = bf16[5120,1536]{1,0:T(8,128)(2,1)} async-done(((bf16[320,1536]{1,0:T(8,128)(2,1)}), bf16[5120,1536]{1,0:T(8,128)(2,1)}) %all-gather.11.cloned.1.call-update) | async-done | bytes 15728656 | tf_op jit(solution)/shard_map/all_gather | solution.py:96
  177.1 120.8 %all-gather.7.cloned.1.call-done = bf16[5120,1536]{1,0:T(8,128)(2,1)} async-done(((bf16[320,1536]{1,0:T(8,128)(2,1)}), bf16[5120,1536]{1,0:T(8,128)(2,1)}) %all-gather.7.cloned.1.call-update) | async-done | bytes 15728656 | tf_op jit(solution)/shard_map/all_gather | solution.py:94
  297.9 120.7 %all-gather.9.cloned.1.call-done = bf16[5120,1536]{1,0:T(8,128)(2,1)} async-done(((bf16[320,1536]{1,0:T(8,128)(2,1)}), bf16[5120,1536]{1,0:T(8,128)(2,1)}) %all-gather.9.cloned.1.call-update) | async-done | bytes 15728656 | tf_op jit(solution)/shard_map/all_gather | solution.py:95
  418.6 21.9 %fusion.15 = f32[256,4608]{1,0:T(8,128)} fusion(bf16[256,5120]{1,0:T(8,128)(2,1)} %all-gather.5.cloned.1.call-done, bf16[5120,1536]{1,0:T(8,128)(2,1)} %all-gather.11.cloned.1.call-done, bf16[5120,1536]{1,0:T(8,128)(2,1)} %all-gather.9.cloned.1.call-done, bf16[5120,1536]{1,0:T(8,128)(2,1)} %all-gather.7.cloned.1.call-done), kind=kOutput, calls=%fused_computation.22 | convolution fusion | flops 12221153280 | bytes 54525952 | tf_op jit(solution)/shard_map/dot_general | solution.py:99
  440.5 2.2 multiply_reduce_fusion
  442.7 4.9 all-reduce
  447.7 2.2 multiply_convert_fusion
  449.9 1.3 collective-permute-start
  451.3 1.5 slice.25
  452.8 4.1 collective-permute-start.1
  457.0 1.2 copy.20
  458.2 61.4 %all-reduce.4.cloned.1.call-done = (bf16[256,1536]{1,0:T(8,128)(2,1)}, bf16[256,1536]{1,0:T(8,128)(2,1)}) async-done(((bf16[256,1536]{1,0:T(8,128)(2,1)}, bf16[256,1536]{1,0:T(8,128)(2,1)}), (bf16[256,1536]{1,0:T(8,128)(2,1)}, bf16[256,1536]{1,0:T(8,128)(2,1)})) %all-reduce.4.cloned.1.call-update) | async-done | bytes 1572880 | tf_op jit(solution)/shard_map/psum | solution.py:19
  519.6 0.9 copy-done.2
  520.5 1.8 pad_maximum_fusion
  522.3 2.5 copy.21
  524.7 1.5 pad_maximum_fusion.1
  526.2 2.4 copy.22
  528.7 45.7 %while.10 = (s32[]{:T(128)}, bf16[12,256,128]{1,2,0:T(8,128)(2,1)}, s32[12,2,6]{2,1,0:T(2,128)S(1)}, bf16[12,256,128]{1,2,0:T(8,128)(2,1)}, bf16[12,768,128]{1,2...) while((s32[]{:T(128)}, bf16[12,256,128]{1,2,0:T(8,128)(2,1)}, s32[12,2,6]{2,1,0:T(2,128)S(1)}, ...), condition=%wide.region_11.12_spmd, body=%wide.region_8.11_spmd.sunk | while | flops 102104592 | bytes 3552409 | solution.py:72
  528.8 1.4 fusion.38
  530.5 1.3 fusion.40
  531.9 0.6 constant_dynamic-update-slice_fusion.2
  532.6 1.4 fusion.38
  534.3 1.3 fusion.40
  535.7 0.6 constant_dynamic-update-slice_fusion.2
  536.5 1.4 fusion.38
  538.1 1.3 fusion.40
  539.5 0.6 constant_dynamic-update-slice_fusion.2
  540.3 1.4 fusion.38
  541.9 1.3 fusion.40
  543.3 0.6 constant_dynamic-update-slice_fusion.2
  544.1 1.4 fusion.38
  545.7 1.3 fusion.40
  547.1 0.6 constant_dynamic-update-slice_fusion.2
  547.9 1.4 fusion.38
  549.5 1.3 fusion.40
  550.9 0.6 constant_dynamic-update-slice_fusion.2
  551.7 1.4 fusion.38
  553.3 1.3 fusion.40
  554.7 0.6 constant_dynamic-update-slice_fusion.2
  555.5 1.4 fusion.38
  557.1 1.3 fusion.40
  558.5 0.6 constant_dynamic-update-slice_fusion.2
  559.3 1.4 fusion.38
  560.9 1.3 fusion.40
  562.3 0.6 constant_dynamic-update-slice_fusion.2
  563.1 1.4 fusion.38
  564.7 1.3 fusion.40
  566.1 0.6 constant_dynamic-update-slice_fusion.2
  566.9 1.4 fusion.38
  568.6 1.3 fusion.40
  570.0 0.6 constant_dynamic-update-slice_fusion.2
  570.8 1.4 fusion.38
  572.4 1.3 fusion.40
  573.8 0.6 constant_dynamic-update-slice_fusion.2
  574.4 2.3 copy.27
  (111 shorter events, 6.9 us)
Async XLA Ops:
  6.5 4.3 copy-start
  6.5 4.2 copy-start.6
  6.5 4.3 copy-start.5
  6.5 47.9 %all-gather.5.cloned.1.call-start = ((), (), s32[]{:S(2)}) async-start(), calls=%async_computation | async-start | bytes 3932160 | tf_op jit(solution)/shard_map/all_gather | solution.py:100
  12.6 2.1 copy-start.10
  12.6 3.4 copy-start.3
  12.6 3.4 copy-start.4
  12.6 164.5 %all-gather.11.cloned.1.call-start = ((), (), s32[]{:S(2)}) async-start(), calls=%async_computation.3 | async-start | bytes 16711680 | tf_op jit(solution)/shard_map/all_gather | solution.py:96
  13.4 284.6 %all-gather.7.cloned.1.call-start = ((), (), s32[]{:S(2)}) async-start(), calls=%async_computation.1 | async-start | bytes 16711680 | tf_op jit(solution)/shard_map/all_gather | solution.py:94
  14.1 404.5 %all-gather.9.cloned.1.call-start = ((), (), s32[]{:S(2)}) async-start(), calls=%async_computation.2 | async-start | bytes 16711680 | tf_op jit(solution)/shard_map/all_gather | solution.py:95
  14.7 504.9 %all-reduce.4.cloned.1.call-start = ((), (), s32[]{:S(2)}) async-start(), calls=%async_computation.4 | async-start | bytes 3145728 | tf_op jit(solution)/shard_map/psum | solution.py:19
  440.5 7.2 %copy-start.7 = (f32[1536]{0:T(1024)S(1)}, f32[1536]{0:T(1024)}, u32[]{:S(2)}) copy-start(f32[1536]{0:T(1024)} %param.23) | copy-start | bytes 18436
  440.5 7.2 %copy-start.8 = (f32[1536]{0:T(1024)S(1)}, f32[1536]{0:T(1024)}, u32[]{:S(2)}) copy-start(f32[1536]{0:T(1024)} %param.22) | copy-start | bytes 18436
  447.7 9.2 %copy-start.9 = (s32[12,2,6]{0,1,2:T(2,128)S(1)}, s32[12,2,6]{0,1,2:T(2,128)}, u32[]{:S(2)}) copy-start(s32[12,2,6]{0,1,2:T(2,128)} %param.27) | copy-start | bytes 1732
  449.9 69.7 %copy-start.1 = (bf16[256,1536]{1,0:T(8,128)(2,1)}, bf16[256,1536]{1,0:T(8,128)(2,1)S(1)}, u32[]{:S(2)}) copy-start(bf16[256,1536]{1,0:T(8,128)(2,1)S(1)} %get-tuple-element.82) | copy-start | bytes 2359300
  449.9 69.7 %collective-permute-start = (bf16[256,1536]{1,0:T(8,128)(2,1)S(1)}, bf16[256,1536]{1,0:T(8,128)(2,1)S(1)}, u32[]{:S(2)}, u32[]{:S(2)}) collective-permute-start(bf16[256,1536]{1,0:T(8,128)(2,1)S(1)} %get-tuple-element.82), channel_id=1, source_target_pairs={{0,2},{2,4},{4,6},{6,8},{8,10},{10,12},{12,14},{14,16},{16,18},{18... | collective-permute-start | bytes 2359304 | tf_op jit(solution)/shard_map/ppermute | solution.py:14
  452.8 71.9 %collective-permute-start.1 = (bf16[256,1536]{1,0:T(8,128)(2,1)S(1)}, bf16[256,1536]{1,0:T(8,128)(2,1)}, u32[]{:S(2)}, u32[]{:S(2)}) collective-permute-start(bf16[256,1536]{1,0:T(8,128)(2,1)S(1)} %slice.25), channel_id=1, source_target_pairs={{0,2},{2,4},{4,6},{6,8},{8,10},{10,12},{12,14},{14,16},{16,18},{18... | collective-permute-start | bytes 2359304 | tf_op jit(solution)/shard_map/ppermute | solution.py:14
  519.6 0.9 copy-start.2
Sparse Core Ops, SparseCore 0:
  12.7 41.7 all-gather.4
  56.8 120.2 all-gather.10
  179.4 118.4 all-gather.6
  300.1 118.4 all-gather.8
  422.0 97.5 all-reduce.3
where the time goes:
time: 584 us; the launch traced here: 583 us
  waiting for transfers between devices  465 us (80%)
  matrix products  53.4 us (9%)
  local copies, waits for them, and re-layouts  22 us (4%)
  other arithmetic  17.7 us (3%)
  between operations  14.7 us (3%)
    all_gather x1, waiting for transfers between devices, local(): lax.all_gather(w_value, 'group', axis=0, tiled=True)  123 us
    all_gather x1, waiting for transfers between devices, local(): lax.all_gather(w_query, 'group', axis=0, tiled=True)  121 us
    all_gather x1, waiting for transfers between devices, local(): lax.all_gather(w_key, 'group', axis=0, tiled=True)  121 us
    psum x1, waiting for transfers between devices, spread_2(): return lax.psum(kept, axis)  61.4 us
    all_gather x1, waiting for transfers between devices, local(): lax.all_gather(modulated, 'tok', axis=0, tiled=True)  37.2 us
    dot_general x1, matrix products, local(): jnp.dot(lax.all_gather(modulated, 'tok', axis=0, tiled=True), joined, pre...  21.9 us
    dot_general x12, matrix products, one_block(): jnp.einsum('id,jd->ij', block_queries, key_head, preferred_element_type=j...  16.2 us
    dot_general x12, matrix products, one_block(): jnp.dot(weights.astype(jnp.bfloat16), value_head, preferred_element_type=...  15.2 us
  transfers between devices with their start and end apart: 7, of which 5 were waited for; matrix products, arithmetic and copies ran while one was open for 6% of the time, Pallas kernels for 0%

commit v1 on v0

--- a/solution.py
+++ b/solution.py
@@ -1,11 +1,15 @@
+import functools
 import math
 
 import jax
 import jax.numpy as jnp
 from jax import lax
+from jax.experimental import pallas as pl
+from jax.experimental.pallas import tpu as pltpu
 from jax.sharding import PartitionSpec as P
 
 EPSILON = 1e-06
+MESH = pl.DeviceIdType.MESH
 
 
 def from_behind(block, axis, distance):
@@ -133,25 +137,301 @@
     return attended.transpose(1, 0, 2).reshape(group_rows, head_cols)
 
 
+AXES = ("zh", "zl", "y", "c", "x")
+
+
+def gather_kernel(wq_ref, wk_ref, wv_ref, m_ref, gw_ref, ga_ref, ws, wr, ys, yr, as_, ar, ls):
+    zh, zl, y, c, x = (lax.axis_index(a) for a in AXES)
+    weights = (wq_ref, wk_ref, wv_ref)
+    rows = wq_ref.shape[0]
+    cols = gw_ref.shape[2] // 3
+
+    def flipped(f):
+        return (
+            1 - zh if f & 4 else zh,
+            1 - zl if f & 2 else zl,
+            1 - c if f & 1 else c,
+        )
+
+    def place(fzh, fzl, fy, fc):
+        return ((fzh * 2 + fzl) * 2 + fy) * 2 + fc
+
+    barrier = pltpu.get_barrier_semaphore()
+    partners = [(a, b, y, d, x) for a, b, d in map(flipped, range(1, 8))]
+    partners += [(zh, zl, 1 - y, c, x), (zh, zl, y, c, 1 - x)]
+    for partner in partners:
+        pl.semaphore_signal(barrier, inc=1, device_id=partner, device_id_type=MESH)
+    pl.semaphore_wait(barrier, len(partners))
+
+    me = place(zh, zl, y, c)
+    wcopies = {}
+
+    def start_weights(f):
+        a, b, d = flipped(f)
+        slab = (b * 2 + d) * cols
+        out = []
+        for t in range(3):
+            src = weights[t].at[:, pl.ds(pl.multiple_of(slab, 128), cols)]
+            dst = gw_ref.at[me, :, pl.ds(t * cols, cols)]
+            if f == 0:
+                cp = pltpu.make_async_copy(src, dst, wr.at[f, t])
+            else:
+                cp = pltpu.make_async_remote_copy(
+                    src_ref=src,
+                    dst_ref=dst,
+                    send_sem=ws.at[f, t],
+                    recv_sem=wr.at[f, t],
+                    device_id=(a, b, y, d, x),
+                    device_id_type=MESH,
+                )
+            cp.start()
+            out.append(cp)
+        wcopies[f] = out
+
+    ycopies = []
+
+    def forward(f):
+        for cp in wcopies[f]:
+            if f == 0:
+                cp.wait()
+            else:
+                cp.wait_recv()
+        a, b, d = flipped(f)
+        slot = place(a, b, y, d)
+        cp = pltpu.make_async_remote_copy(
+            src_ref=gw_ref.at[slot],
+            dst_ref=gw_ref.at[slot],
+            send_sem=ys.at[f],
+            recv_sem=yr.at[f],
+            device_id=(zh, zl, 1 - y, c, x),
+            device_id_type=MESH,
+        )
+        cp.start()
+        ycopies.append(cp)
+
+    acopies = {}
+
+    def start_tokens(k, src, slot, target):
+        cp = pltpu.make_async_remote_copy(
+            src_ref=src,
+            dst_ref=ga_ref.at[slot],
+            send_sem=as_.at[k],
+            recv_sem=ar.at[k],
+            device_id=target,
+            device_id_type=MESH,
+        )
+        cp.start()
+        acopies[k] = cp
+
+    def token_slot(b, d, e):
+        return (b * 2 + d) * 2 + e
+
+    to_z, to_x, to_c = (zh, 1 - zl, y, c, x), (zh, zl, y, c, 1 - x), (zh, zl, y, 1 - c, x)
+    mine = token_slot(zl, c, x)
+    start_tokens(0, m_ref, mine, to_z)
+    start_weights(0)
+    start_weights(1)
+    start_weights(4)
+    start_tokens(1, m_ref, mine, to_x)
+    start_tokens(2, m_ref, mine, to_c)
+    local = pltpu.make_async_copy(m_ref, ga_ref.at[mine], ls.at[0])
+    local.start()
+    start_weights(5)
+    forward(0)
+    forward(1)
+    acopies[0].wait_recv()
+    theirs = token_slot(1 - zl, c, x)
+    start_tokens(3, ga_ref.at[theirs], theirs, to_x)
+    start_tokens(4, ga_ref.at[theirs], theirs, to_c)
+    start_weights(2)
+    forward(4)
+    start_weights(6)
+    start_weights(3)
+    acopies[1].wait_recv()
+    across = token_slot(zl, c, 1 - x)
+    start_tokens(5, ga_ref.at[across], across, to_c)
+    forward(2)
+    forward(5)
+    start_weights(7)
+    acopies[3].wait_recv()
+    far = token_slot(1 - zl, c, 1 - x)
+    start_tokens(6, ga_ref.at[far], far, to_c)
+    forward(3)
+    forward(6)
+    forward(7)
+    local.wait()
+    for k in (2, 4, 5, 6):
+        acopies[k].wait_recv()
+    for cp in ycopies:
+        cp.wait_recv()
+    for f in range(1, 8):
+        for cp in wcopies[f]:
+            cp.wait_send()
+    for cp in ycopies:
+        cp.wait_send()
+    for k in range(7):
+        acopies[k].wait_send()
+
+
+def gather_operands(w_query, w_key, w_value, modulated):
+    rows, half = w_query.shape
+    tokens, width = modulated.shape
+    dma = pltpu.SemaphoreType.DMA
+    anywhere = pl.BlockSpec(memory_space=pl.ANY)
+    gw, ga = pl.pallas_call(
+        gather_kernel,
+        out_shape=(
+            jax.ShapeDtypeStruct((16, rows, 3 * half // 4), w_query.dtype),
+            jax.ShapeDtypeStruct((8, tokens, width), modulated.dtype),
+        ),
+        in_specs=[anywhere] * 4,
+        out_specs=(anywhere, anywhere),
+        scratch_shapes=[dma((8, 3)), dma((8, 3)), dma((8,)), dma((8,)), dma((7,)), dma((7,)), dma((1,))],
+        compiler_params=pltpu.CompilerParams(collective_id=0, has_side_effects=True),
+        cost_estimate=pl.CostEstimate(flops=0, bytes_accessed=400_000_000, transcendentals=0),
+    )(w_query, w_key, w_value, modulated)
+    return gw.reshape(16 * rows, 3 * half // 4), ga.reshape(8 * tokens, width)
+
+
+def attend_kernel(
+    mask_ref, q_ref, k_ref, v_ref, kp_ref, vp_ref, ke_ref, ve_ref, kc_ref, vc_ref, o_ref, *, scale, tile, qtiles, ktiles
+):
+    g, h = pl.program_id(0), pl.program_id(1)
+    own = g % 2 == 1
+    k_prev = jnp.where(own, kp_ref[...], ke_ref[...])
+    v_prev = jnp.where(own, vp_ref[...], ve_ref[...])
+    keys = jnp.concatenate([kc_ref[...], k_prev, k_ref[...]], axis=0)
+    vals = jnp.concatenate([vc_ref[...], v_prev, v_ref[...]], axis=0)
+    for i in range(qtiles):
+        q = q_ref[i * tile : (i + 1) * tile, :]
+        s = lax.dot_general(q, keys, (((1,), (1,)), ((), ())), preferred_element_type=jnp.float32) * scale
+        parts = []
+        for j in range(ktiles):
+            seen = mask_ref[((g * pl.num_programs(1) + h) * qtiles + i) * ktiles + j]
+            parts.append(jnp.where(seen > 0, s[:, j * tile : (j + 1) * tile], -jnp.inf))
+        s = jnp.concatenate(parts, axis=1)
+        peak = jnp.max(s, axis=-1, keepdims=True)
+        w = jnp.exp(s - peak)
+        total = jnp.sum(w, axis=-1, keepdims=True)
+        summed = jnp.dot(w.astype(jnp.bfloat16), vals, preferred_element_type=jnp.float32)
+        o_ref[i * tile : (i + 1) * tile, :] = (summed / total).astype(jnp.bfloat16)
+
+
+def attend(mask, q, k, v, k_edge, v_edge, k_cache, v_cache, scale, rows, head, qtiles, ktiles):
+    groups, heads = q.shape[0] // rows, q.shape[1] // head
+    cur = pl.BlockSpec((rows, head), lambda g, h: (g, h))
+    prev = pl.BlockSpec((rows, head), lambda g, h: (jnp.maximum(g - 1, 0), h))
+    edge = pl.BlockSpec((rows, head), lambda g, h: (g // 2, h))
+    cache = pl.BlockSpec((rows, head), lambda g, h: (0, h))
+    return pl.pallas_call(
+        functools.partial(attend_kernel, scale=scale, tile=rows // qtiles, qtiles=qtiles, ktiles=ktiles),
+        grid=(groups, heads),
+        out_shape=jax.ShapeDtypeStruct(q.shape, jnp.bfloat16),
+        in_specs=[pl.BlockSpec(memory_space=pltpu.SMEM), cur, cur, cur, prev, prev, edge, edge, cache, cache],
+        out_specs=cur,
+    )(mask, q, k, v, k, v, k_edge, v_edge, k_cache, v_cache)
+
+
+def local_split(
+    latents,
+    timesteps,
+    mod_shift,
+    mod_scale,
+    w_query,
+    w_key,
+    w_value,
+    query_gain,
+    key_gain,
+    cache_keys,
+    cache_values,
+    owners,
+    tile_mask,
+):
+    zh, zl, y, c, x = (lax.axis_index(a) for a in AXES)
+    member = ((zh * 2 + zl) * 2 + y) * 2 + c
+    modulated = modulate(latents, timesteps[0], mod_shift, mod_scale)
+    root = owners[owners.shape[0] - 1]
+    kept = jnp.where(member == root, jnp.concatenate([cache_keys, cache_values], axis=1), 0)
+    cached = lax.psum(kept.astype(jnp.bfloat16), ("zh", "zl", "y", "c"))
+    joined, tokens = gather_operands(w_query, w_key, w_value, modulated)
+    half = w_query.shape[1]
+    cols = half // 4
+    slab = (zl * 2 + c) * cols
+    projected = jnp.dot(tokens, joined, preferred_element_type=jnp.float32)
+    raw_query = projected[:, :cols]
+    raw_key = projected[:, cols : 2 * cols]
+    raw_value = projected[:, 2 * cols :]
+    squares = lax.psum(
+        jnp.stack([jnp.sum(raw_query * raw_query, axis=1), jnp.sum(raw_key * raw_key, axis=1)]),
+        ("zl", "c", "x"),
+    )
+    width = 2 * half
+    q_gain = lax.dynamic_slice_in_dim(query_gain, slab, cols, 0)
+    k_gain = lax.dynamic_slice_in_dim(key_gain, slab, cols, 0)
+    query_rows = scaled_rows(raw_query, squares[0], width, q_gain)
+    key_rows = scaled_rows(raw_key, squares[1], width, k_gain)
+    value_rows = raw_value.astype(jnp.bfloat16)
+    rows = query_rows.shape[0] // 4
+    tails = [jnp.concatenate([a[s * rows : (s + 1) * rows] for a in (key_rows, value_rows)], axis=1) for s in (1, 3)]
+    swapped = lax.ppermute(tails[0], "y", [(0, 1), (1, 0)])
+    shifted = lax.ppermute(tails[1], ("zh", "y"), [(0, 1), (1, 2), (2, 3)])
+    edges = jnp.concatenate(
+        [jnp.where(y == 0, shifted, swapped), jnp.where(y == 0, swapped, shifted)], axis=0
+    )
+    heads = tile_mask.shape[0] // 4
+    query_tiles, key_tiles = tile_mask.shape[1:]
+    head = cols // heads
+    mask = lax.dynamic_slice_in_dim(tile_mask, (zl * 2 + c) * heads, heads, 0)
+    slots = jnp.arange(4)
+    group_ids = ((zh * 2 + slots // 2) * 2 + y) * 2 + slots % 2
+    tile_ids = jnp.arange(key_tiles)
+    earlier = (tile_ids >= query_tiles) & (tile_ids < 2 * query_tiles)
+    allowed = jnp.where(
+        (group_ids == 0)[:, None, None, None] & earlier[None, None, None, :], 0, mask[None]
+    ).reshape(-1)
+    attended = attend(
+        allowed,
+        query_rows,
+        key_rows,
+        value_rows,
+        edges[:, :cols],
+        edges[:, cols:],
+        lax.dynamic_slice_in_dim(cached, slab, cols, 1),
+        lax.dynamic_slice_in_dim(cached, half + slab, cols, 1),
+        1.0 / math.sqrt(head),
+        rows,
+        head,
+        query_tiles,
+        key_tiles,
+    )
+    out = lax.all_to_all(attended.reshape(4, rows, cols), ("zl", "c"), split_axis=0, concat_axis=2, tiled=True)
+    return out.reshape(rows, half)
+
+
 def solution(mesh):
+    body, group, tok = local, "group", "tok"
+    if mesh.shape["group"] == 16 and mesh.shape["tok"] == 2:
+        mesh = jax.sharding.Mesh(mesh.devices.reshape(2, 2, 2, 2, 2), AXES)
+        body, group, tok = local_split, ("zh", "zl", "y", "c"), "x"
+    both = (*group, tok) if body is local_split else (group, tok)
     return jax.shard_map(
-        local,
+        body,
         mesh=mesh,
         in_specs=(
-            P(("group", "tok"), None),
-            P("group"),
+            P(both, None),
+            P(group),
             P(),
             P(),
-            P("group", "tok"),
-            P("group", "tok"),
-            P("group", "tok"),
-            P("tok"),
-            P("tok"),
-            P("group", "tok"),
-            P("group", "tok"),
+            P(group, tok),
+            P(group, tok),
+            P(group, tok),
+            P(tok),
+            P(tok),
+            P(group, tok),
+            P(group, tok),
             P(),
-            P("tok", None, None),
+            P(tok, None, None),
         ),
-        out_specs=P("group", "tok"),
+        out_specs=P(group, tok),
         check_vma=False,
     )

time: 584 us -> 360 us (0.62)
  waiting for transfers between devices: 465 us -> 88.8 us
  Pallas kernels: 0 us -> 179 us
  matrix products: 53.4 us -> 17.3 us
  blocking collectives: 4.94 us -> 29.8 us
  local copies, waits for them, and re-layouts: 22 us -> 11.5 us
    all_gather x4 -> x0, waiting for transfers between devices: 401 us -> none  [the longest x1 123 us: local(): lax.all_gather(w_value, 'group', axis=0, tiled=True)]
    pallas_call x0 -> x2, Pallas kernels: none -> 179 us  [the longest x1 165 us: gather_operands(): pl.pallas_call(gather_kernel, out_shape=(jax.ShapeDtypeStruct((16, rows,...]
    dot_general x25 -> x1, matrix products: 53.4 us -> 17.3 us  [local_split(): projected = jnp.dot(tokens, joined, preferred_element_type=jnp.float32)]
    psum x1, waiting for transfers between devices: 61.4 us -> 80 us  [local_split(): cached = lax.psum(kept.astype(jnp.bfloat16), ('zh', 'zl', 'y', 'c'))]
    all_to_all x0 -> x1, blocking collectives: none -> 15.1 us  [local_split(): lax.all_to_all(attended.reshape(4, rows, cols), ('zl', 'c'), split_axis=0...]
    psum x1, blocking collectives: 4.94 us -> 14.7 us  [local_split(): lax.psum(jnp.stack([jnp.sum(raw_query * raw_query, axis=1), jnp.sum(raw_k...]
    dynamic_update_slice x24 -> x0, local copies, waits for them, and re-layouts: 8.86 us -> none  [dense_attention(): return lax.map(one_head, (query_heads, key_heads, value_heads, allowed))]
    ppermute x2, waiting for transfers between devices: 0.01 us -> 8.8 us  [the longest x1 8.8 us: local_split(): shifted = lax.ppermute(tails[1], ('zh', 'y'), [(0, 1), (1, 2), (2, 3)])]
  transfers between devices with their start and end apart: 7 -> 3, of which waited for: 5 -> 2; matrix products, arithmetic and copies ran while one was open for 6% -> 2% of each run, Pallas kernels for 0% -> 0%
where the time goes in v1:
time: 360 us; the launch traced here: 358 us
  Pallas kernels  179 us (50%)
  waiting for transfers between devices  88.8 us (25%)
  blocking collectives  29.8 us (8%)
  matrix products  17.3 us (5%)
  between operations  15 us (4%)
  other arithmetic  12.6 us (4%)
  local copies, waits for them, and re-layouts  11.5 us (3%)
  starting transfers between devices  4.77 us (1%)
    pallas_call x1, Pallas kernels, gather_operands(): pl.pallas_call(gather_kernel, out_shape=(jax.ShapeDtypeStruct((16, rows,...  165 us
    psum x1, waiting for transfers between devices, local_split(): cached = lax.psum(kept.astype(jnp.bfloat16), ('zh', 'zl', 'y', 'c'))  80 us
    dot_general x1, matrix products, local_split(): projected = jnp.dot(tokens, joined, preferred_element_type=jnp.float32)  17.3 us
    all_to_all x1, blocking collectives, local_split(): lax.all_to_all(attended.reshape(4, rows, cols), ('zl', 'c'), split_axis=0...  15.1 us
    psum x1, blocking collectives, local_split(): lax.psum(jnp.stack([jnp.sum(raw_query * raw_query, axis=1), jnp.sum(raw_k...  14.7 us
    pallas_call x1, Pallas kernels, attend(): pl.pallas_call(functools.partial(attend_kernel, scale=scale, tile=rows //...  13.2 us
    ppermute x1, waiting for transfers between devices, local_split(): shifted = lax.ppermute(tails[1], ('zh', 'y'), [(0, 1), (1, 2), (2, 3)])  8.8 us
  transfers between devices with their start and end apart: 3, of which 2 were waited for; matrix products, arithmetic and copies ran while one was open for 2% of the time, Pallas kernels for 0%

profile of v1, /device:TPU:0, one launch (start us, length us, event | category | flops | bytes accessed | tf_op | source)
XLA Modules:
  0.0 358.4 jit_solution(188436177910904373)
XLA Ops:
  6.5 0.0 copy-start
  6.5 0.0 copy-start.1
  6.5 0.0 copy-start.8
  6.5 0.0 copy-start.7
  6.5 0.0 all-reduce.2.cloned.1.call-start
  7.3 1.6 convert_reduce_fusion
  8.9 1.8 fusion.2
  10.8 0.0 copy-done.8
  10.8 0.1 sine_multiply_fusion
  10.9 0.0 copy-done.1
  10.9 0.0 copy-done.7
  10.9 1.7 fusion.6.m_ref
  12.6 165.5 %shard_map.127 = (bf16[16,320,1152]{2,1,0:T(8,128)(2,1)}, bf16[8,128,5120]{2,1,0:T(8,128)(2,1)}) custom-call(bf16[320,1536]{1,0:T(8,128)(2,1)} %wq_ref.1, bf16[320,1536]{1,0:T(8,128)(2,1)} %wk_ref.1, bf16[320,1536]{1,0:T(8,128)(2,1)} %wv_ref.1, bf16[128,5120]{1,0:T(8,128)(2,1)} %fusion.6.m_ref), custom_call_target="tpu_custom_call" | custom-call | bytes 400000000 | tf_op jit(solution)/shard_map/pallas_call | solution.py:281
  178.1 17.3 %fusion.20 = (bf16[1024,1152]{1,0:T(8,128)(2,1)S(1)}, f32[1024,1152]{1,0:T(8,128)S(1)}) fusion(bf16[1024,5120]{1,0:T(8,128)(2,1)} %bitcast.25, bf16[5120,1152]{1,0:T(8,128)(2,1)} %bitcast.24), kind=kOutput, calls=%fused_computation.53 | convolution fusion | flops 12080775168 | bytes 29360128 | tf_op jit(solution)/shard_map/dot_general | solution.py:360
  195.4 0.0 copy-start.3
  195.4 0.0 copy-start.6
  195.4 2.1 copy-done.3
  197.6 0.3 multiply_reduce_fusion.1
  197.9 14.7 %psum.14 = f32[2,1024]{1,0:T(2,128)S(1)} all-reduce(f32[2,1024]{1,0:T(2,128)S(1)} %pad_maximum_fusion.3), channel_id=1, replica_groups=mesh['zh'=2,'zl'=2,'y'=2,'c'=2,'x'=2] {'zl','c','x'}, use_global_device_ids=true, to_apply=%region_4.5 | all-reduce | flops 2048 | bytes 16384 | tf_op jit(solution)/shard_map/psum | solution.py:364
  212.6 0.8 dynamic_slice.17
  213.4 0.8 dynamic_slice.16
  214.2 0.0 copy-done.6
  214.2 0.0 copy-start.4
  214.2 0.0 copy-start.5
  214.3 3.2 multiply_convert_fusion
  217.5 0.0 copy-start.2
  217.6 0.1 collective-permute-start.1
  217.7 4.7 %collective-permute-start = (bf16[256,768]{1,0:T(8,128)(2,1)S(1)}, bf16[256,768]{1,0:T(8,128)(2,1)}, u32[]{:S(2)}, u32[]{:S(2)}) collective-permute-start(bf16[256,768]{1,0:T(8,128)(2,1)S(1)} %pad_maximum_fusion.1), channel_id=1, source_target_pairs={{0,4},{4,16},{16,20},{1,5},{5,17},{17,21},{2,6},{6,18},{18,22},{3,... | collective-permute-start | bytes 1179656 | tf_op jit(solution)/shard_map/ppermute | solution.py:377
  222.4 1.3 slice.50
  224.3 0.0 copy-done.4
  224.3 0.0 copy-done.5
  224.3 1.5 maximum_select_fusion
  225.8 0.0 copy-done.2
  225.8 0.0 all-reduce.2.cloned.1.call-update
  225.9 2.1 slice.55.v_ref.vp_ref
  228.0 0.0 copy-done
  228.0 0.1 constant_dynamic-slice_fusion.2
  228.0 0.1 copy.14
  228.1 0.1 broadcast_and_fusion
  228.2 0.7 select_n.65.mask_ref
  228.9 0.0 collective-permute-done.1
  228.9 8.8 %collective-permute-done = bf16[256,768]{1,0:T(8,128)(2,1)} collective-permute-done((bf16[256,768]{1,0:T(8,128)(2,1)S(1)}, bf16[256,768]{1,0:T(8,128)(2,1)}, u32[]{:S(2)}, u32[]{:S(2)}) %collective-permute-start) | collective-permute-done | bytes 393248 | tf_op jit(solution)/shard_map/ppermute | solution.py:377
  237.7 1.1 broadcast_select_fusion
  238.8 1.0 pad_maximum_fusion
  239.8 80.0 %all-reduce.2.cloned.1.call-done = bf16[256,3072]{1,0:T(8,128)(2,1)} async-done(((bf16[256,3072]{1,0:T(8,128)(2,1)}), bf16[256,3072]{1,0:T(8,128)(2,1)}) %all-reduce.2.cloned.1.call-update) | async-done | bytes 1572880 | tf_op jit(solution)/shard_map/psum | solution.py:355
  319.8 1.8 constant_dynamic-slice_fusion
  321.6 13.2 %shard_map.128 = bf16[1024,384]{1,0:T(8,128)(2,1)} custom-call(s32[144]{0:T(256)} %select_n.65.mask_ref, bf16[1024,384]{1,0:T(8,128)(2,1)} %get-tuple-element.12.q_ref, bf16[1024,384]{1,0:T(8,128)(2,1)} %copy-done.2, bf16[1024,384]{1,0:T(8,128)(2,1)} %slice.55.v_ref.vp_ref, bf16[1024,384]{1,0:T(8,128)(2,1)} %copy-done.2, ...), custom_call_target="tpu_custom_call" | custom-call | tf_op jit(solution)/shard_map/pallas_call | solution.py:326
  334.8 15.1 %all_to_all.15 = bf16[4,256,384]{2,1,0:T(8,128)(2,1)S(1)} all-to-all(bf16[4,256,384]{2,1,0:T(8,128)(2,1)} %bitcast.17), channel_id=1, replica_groups=mesh['zh'=2,'zl'=2,'y'=2,'c'=2,'x'=2] {'zl','c'}, dimensions={0} | all-to-all | bytes 1572864 | tf_op jit(solution)/shard_map/all_to_all | solution.py:407
  350.0 0.6 copy.15
  350.6 1.0 copy.16
  (11 shorter events, 0.2 us)
Async XLA Ops:
  6.5 221.4 %copy-start = (s32[12,2,6]{0,1,2:T(2,128)S(1)}, s32[12,2,6]{0,1,2:T(2,128)}, u32[]{:S(2)}) copy-start(s32[12,2,6]{0,1,2:T(2,128)} %param.25) | copy-start | bytes 1732
  6.5 4.3 %copy-start.1 = (bf16[128,5120]{1,0:T(8,128)(2,1)S(1)}, bf16[128,5120]{1,0:T(8,128)(2,1)}, u32[]{:S(2)}) copy-start(bf16[128,5120]{1,0:T(8,128)(2,1)} %param.13) | copy-start | bytes 3932164
  6.5 4.2 %copy-start.8 = (f32[5120]{0:T(1024)S(1)}, f32[5120]{0:T(1024)}, u32[]{:S(2)}) copy-start(f32[5120]{0:T(1024)} %param.16) | copy-start | bytes 61444
  6.5 4.4 %copy-start.7 = (f32[5120]{0:T(1024)S(1)}, f32[5120]{0:T(1024)}, u32[]{:S(2)}) copy-start(f32[5120]{0:T(1024)} %param.15) | copy-start | bytes 61444
  6.5 313.2 %all-reduce.2.cloned.1.call-start = ((), (), s32[]{:S(2)}) async-start(), calls=%async_computation.1 | async-start | bytes 3145728 | tf_op jit(solution)/shard_map/psum | solution.py:355
  195.4 2.1 copy-start.3
  195.4 18.8 %copy-start.6 = (bf16[1024,1152]{1,0:T(8,128)(2,1)}, bf16[1024,1152]{1,0:T(8,128)(2,1)S(1)}, u32[]{:S(2)}) copy-start(bf16[1024,1152]{1,0:T(8,128)(2,1)S(1)} %get-tuple-element.25) | copy-start | bytes 7077892
  214.2 10.1 %copy-start.4 = (bf16[256,1536]{1,0:T(8,128)(2,1)S(1)}, bf16[256,1536]{1,0:T(8,128)(2,1)}, u32[]{:S(2)}) copy-start(bf16[256,1536]{1,0:T(8,128)(2,1)} %param.23) | copy-start | bytes 2359300
  214.2 10.1 %copy-start.5 = (bf16[256,1536]{1,0:T(8,128)(2,1)S(1)}, bf16[256,1536]{1,0:T(8,128)(2,1)}, u32[]{:S(2)}) copy-start(bf16[256,1536]{1,0:T(8,128)(2,1)} %param.22) | copy-start | bytes 2359300
  217.5 8.3 %copy-start.2 = (bf16[1024,384]{1,0:T(8,128)(2,1)}, bf16[1024,384]{1,0:T(8,128)(2,1)S(1)}, u32[]{:S(2)}) copy-start(bf16[1024,384]{1,0:T(8,128)(2,1)S(1)} %get-tuple-element.11.k_ref.kp_ref) | copy-start | bytes 2359300
  217.6 11.4 %collective-permute-start.1 = (bf16[256,768]{1,0:T(8,128)(2,1)S(1)}, bf16[256,768]{1,0:T(8,128)(2,1)S(1)}, u32[]{:S(2)}, u32[]{:S(2)}) collective-permute-start(bf16[256,768]{1,0:T(8,128)(2,1)S(1)} %pad_maximum_fusion.2), channel_id=1, source_target_pairs={{0,4},{4,0},{1,5},{5,1},{2,6},{6,2},{3,7},{7,3},{8,12},{12,8},{9,1... | collective-permute-start | bytes 1179656 | tf_op jit(solution)/shard_map/ppermute | solution.py:376
  217.7 20.0 %collective-permute-start = (bf16[256,768]{1,0:T(8,128)(2,1)S(1)}, bf16[256,768]{1,0:T(8,128)(2,1)}, u32[]{:S(2)}, u32[]{:S(2)}) collective-permute-start(bf16[256,768]{1,0:T(8,128)(2,1)S(1)} %pad_maximum_fusion.1), channel_id=1, source_target_pairs={{0,4},{4,16},{16,20},{1,5},{5,17},{17,21},{2,6},{6,18},{18,22},{3,... | collective-permute-start | bytes 1179656 | tf_op jit(solution)/shard_map/ppermute | solution.py:377
Sparse Core Ops, SparseCore 0:
  226.0 93.7 all-reduce.1

commit v2 on v1

--- a/solution.py
+++ b/solution.py
@@ -140,7 +140,10 @@
 AXES = ("zh", "zl", "y", "c", "x")
 
 
-def gather_kernel(wq_ref, wk_ref, wv_ref, m_ref, gw_ref, ga_ref, ws, wr, ys, yr, as_, ar, ls):
+def gather_kernel(
+    wq_ref, wk_ref, wv_ref, m_ref, ck_ref, cv_ref, flag_ref, gw_ref, ga_ref, cache_ref,
+    kept, from_c, halves, from_z, part, from_y, from_zh, ws, wr, ys, yr, as_, ar, ls, cs, cr
+):
     zh, zl, y, c, x = (lax.axis_index(a) for a in AXES)
     weights = (wq_ref, wk_ref, wv_ref)
     rows = wq_ref.shape[0]
@@ -226,6 +229,18 @@
     def token_slot(b, d, e):
         return (b * 2 + d) * 2 + e
 
+    def start_cache(k, src, dst, target):
+        cp = pltpu.make_async_remote_copy(
+            src_ref=src,
+            dst_ref=dst,
+            send_sem=cs.at[k],
+            recv_sem=cr.at[k],
+            device_id=target,
+            device_id_type=MESH,
+        )
+        cp.start()
+        return cp
+
     to_z, to_x, to_c = (zh, 1 - zl, y, c, x), (zh, zl, y, c, 1 - x), (zh, zl, y, 1 - c, x)
     mine = token_slot(zl, c, x)
     start_tokens(0, m_ref, mine, to_z)
@@ -238,13 +253,25 @@
     local.start()
     start_weights(5)
     forward(0)
+    for p in range(4):
+        for t, ref in enumerate((ck_ref, cv_ref)):
+            block = ref[:, p * cols : (p + 1) * cols].astype(jnp.float32) * flag_ref[...]
+            kept[p, :, t * cols : (t + 1) * cols] = block.astype(jnp.bfloat16)
+    cache_c = [start_cache(j, kept.at[2 * j + 1 - c], from_c.at[j], to_c) for j in range(2)]
     forward(1)
+    for j in range(2):
+        cache_c[j].wait()
+        halves[j] = kept[2 * j + c] + from_c[j]
+    cache_z = start_cache(2, halves.at[1 - zl], from_z, to_z)
     acopies[0].wait_recv()
     theirs = token_slot(1 - zl, c, x)
     start_tokens(3, ga_ref.at[theirs], theirs, to_x)
     start_tokens(4, ga_ref.at[theirs], theirs, to_c)
     start_weights(2)
     forward(4)
+    cache_z.wait()
+    part[0] = halves[zl] + from_z[...]
+    cache_y = start_cache(3, part.at[0], from_y, (zh, zl, 1 - y, c, x))
     start_weights(6)
     start_weights(3)
     acopies[1].wait_recv()
@@ -253,12 +280,17 @@
     forward(2)
     forward(5)
     start_weights(7)
+    cache_y.wait()
+    part[1] = part[0] + from_y[...]
+    cache_zh = start_cache(4, part.at[1], from_zh, (1 - zh, zl, y, c, x))
     acopies[3].wait_recv()
     far = token_slot(1 - zl, c, 1 - x)
     start_tokens(6, ga_ref.at[far], far, to_c)
     forward(3)
     forward(6)
     forward(7)
+    cache_zh.wait()
+    cache_ref[...] = part[1] + from_zh[...]
     local.wait()
     for k in (2, 4, 5, 6):
         acopies[k].wait_recv()
@@ -273,24 +305,47 @@
         acopies[k].wait_send()
 
 
-def gather_operands(w_query, w_key, w_value, modulated):
+def gather_operands(w_query, w_key, w_value, modulated, cache_keys, cache_values, flag):
     rows, half = w_query.shape
     tokens, width = modulated.shape
     dma = pltpu.SemaphoreType.DMA
     anywhere = pl.BlockSpec(memory_space=pl.ANY)
-    gw, ga = pl.pallas_call(
+    vmem = pl.BlockSpec(memory_space=pltpu.VMEM)
+    slab = (cache_keys.shape[0], half // 2)
+    bf16 = jnp.bfloat16
+    gw, ga, cached = pl.pallas_call(
         gather_kernel,
         out_shape=(
             jax.ShapeDtypeStruct((16, rows, 3 * half // 4), w_query.dtype),
             jax.ShapeDtypeStruct((8, tokens, width), modulated.dtype),
+            jax.ShapeDtypeStruct(slab, bf16),
         ),
-        in_specs=[anywhere] * 4,
-        out_specs=(anywhere, anywhere),
-        scratch_shapes=[dma((8, 3)), dma((8, 3)), dma((8,)), dma((8,)), dma((7,)), dma((7,)), dma((1,))],
-        compiler_params=pltpu.CompilerParams(collective_id=0, has_side_effects=True),
+        in_specs=[anywhere] * 4 + [vmem] * 3,
+        out_specs=(anywhere, anywhere, vmem),
+        scratch_shapes=[
+            pltpu.VMEM((4, *slab), bf16),
+            pltpu.VMEM((2, *slab), bf16),
+            pltpu.VMEM((2, *slab), bf16),
+            pltpu.VMEM(slab, bf16),
+            pltpu.VMEM((2, *slab), bf16),
+            pltpu.VMEM(slab, bf16),
+            pltpu.VMEM(slab, bf16),
+            dma((8, 3)),
+            dma((8, 3)),
+            dma((8,)),
+            dma((8,)),
+            dma((7,)),
+            dma((7,)),
+            dma((1,)),
+            dma((5,)),
+            dma((5,)),
+        ],
+        compiler_params=pltpu.CompilerParams(
+            collective_id=0, has_side_effects=True, vmem_limit_bytes=32 * 1024 * 1024
+        ),
         cost_estimate=pl.CostEstimate(flops=0, bytes_accessed=400_000_000, transcendentals=0),
-    )(w_query, w_key, w_value, modulated)
-    return gw.reshape(16 * rows, 3 * half // 4), ga.reshape(8 * tokens, width)
+    )(w_query, w_key, w_value, modulated, cache_keys, cache_values, flag)
+    return gw.reshape(16 * rows, 3 * half // 4), ga.reshape(8 * tokens, width), cached
 
 
 def attend_kernel(
@@ -317,19 +372,19 @@
         o_ref[i * tile : (i + 1) * tile, :] = (summed / total).astype(jnp.bfloat16)
 
 
-def attend(mask, q, k, v, k_edge, v_edge, k_cache, v_cache, scale, rows, head, qtiles, ktiles):
+def attend(mask, q, k, v, edges, cached, scale, rows, head, qtiles, ktiles):
     groups, heads = q.shape[0] // rows, q.shape[1] // head
     cur = pl.BlockSpec((rows, head), lambda g, h: (g, h))
     prev = pl.BlockSpec((rows, head), lambda g, h: (jnp.maximum(g - 1, 0), h))
-    edge = pl.BlockSpec((rows, head), lambda g, h: (g // 2, h))
-    cache = pl.BlockSpec((rows, head), lambda g, h: (0, h))
+    edge = [pl.BlockSpec((rows, head), lambda g, h, t=t: (g // 2, t * heads + h)) for t in range(2)]
+    cache = [pl.BlockSpec((rows, head), lambda g, h, t=t: (0, t * heads + h)) for t in range(2)]
     return pl.pallas_call(
         functools.partial(attend_kernel, scale=scale, tile=rows // qtiles, qtiles=qtiles, ktiles=ktiles),
         grid=(groups, heads),
         out_shape=jax.ShapeDtypeStruct(q.shape, jnp.bfloat16),
-        in_specs=[pl.BlockSpec(memory_space=pltpu.SMEM), cur, cur, cur, prev, prev, edge, edge, cache, cache],
+        in_specs=[pl.BlockSpec(memory_space=pltpu.SMEM), cur, cur, cur, prev, prev, *edge, *cache],
         out_specs=cur,
-    )(mask, q, k, v, k, v, k_edge, v_edge, k_cache, v_cache)
+    )(mask, q, k, v, k, v, edges, edges, cached, cached)
 
 
 def local_split(
@@ -351,11 +406,12 @@
     member = ((zh * 2 + zl) * 2 + y) * 2 + c
     modulated = modulate(latents, timesteps[0], mod_shift, mod_scale)
     root = owners[owners.shape[0] - 1]
-    kept = jnp.where(member == root, jnp.concatenate([cache_keys, cache_values], axis=1), 0)
-    cached = lax.psum(kept.astype(jnp.bfloat16), ("zh", "zl", "y", "c"))
-    joined, tokens = gather_operands(w_query, w_key, w_value, modulated)
     half = w_query.shape[1]
     cols = half // 4
+    flag = jnp.full((1, cols), member == root, jnp.float32)
+    joined, tokens, cached = gather_operands(
+        w_query, w_key, w_value, modulated, cache_keys, cache_values, flag
+    )
     slab = (zl * 2 + c) * cols
     projected = jnp.dot(tokens, joined, preferred_element_type=jnp.float32)
     raw_query = projected[:, :cols]
@@ -394,10 +450,8 @@
         query_rows,
         key_rows,
         value_rows,
-        edges[:, :cols],
-        edges[:, cols:],
-        lax.dynamic_slice_in_dim(cached, slab, cols, 1),
-        lax.dynamic_slice_in_dim(cached, half + slab, cols, 1),
+        edges,
+        cached,
         1.0 / math.sqrt(head),
         rows,
         head,

time: 360 us -> 277 us (0.77)
  waiting for transfers between devices: 88.8 us -> 10.2 us
  between operations: 15 us -> 1.54 us
  Pallas kernels: 179 us -> 187 us
    psum x1 -> x0, waiting for transfers between devices: 80 us -> none  [local_split(): cached = lax.psum(kept.astype(jnp.bfloat16), ('zh', 'zl', 'y', 'c'))]
    pallas_call x1, Pallas kernels: 165 us -> 174 us  [gather_operands(): pl.pallas_call(gather_kernel, out_shape=(jax.ShapeDtypeStruct((16, rows,...]
    ppermute x1, waiting for transfers between devices: 0.01 us -> 3.78 us  [local_split(): swapped = lax.ppermute(tails[0], 'y', [(0, 1), (1, 0)])]
  transfers between devices with their start and end apart: 3 -> 2, of which waited for: 2 -> 2; matrix products, arithmetic and copies ran while one was open for 2% -> 1% of each run, Pallas kernels for 0% -> 0%
where the time goes in v2:
time: 277 us; the launch traced here: 274 us
  Pallas kernels  187 us (68%)
  blocking collectives  28.9 us (10%)
  matrix products  20.9 us (8%)
  other arithmetic  12.1 us (4%)
  waiting for transfers between devices  10.2 us (4%)
  local copies, waits for them, and re-layouts  8.48 us (3%)
  starting transfers between devices  4.75 us (2%)
    pallas_call x1, Pallas kernels, gather_operands(): pl.pallas_call(gather_kernel, out_shape=(jax.ShapeDtypeStruct((16, rows,...  174 us
    dot_general x1, matrix products, local_split(): projected = jnp.dot(tokens, joined, preferred_element_type=jnp.float32)  20.9 us
    all_to_all x1, blocking collectives, local_split(): lax.all_to_all(attended.reshape(4, rows, cols), ('zl', 'c'), split_axis=0...  15.1 us
    psum x1, blocking collectives, local_split(): lax.psum(jnp.stack([jnp.sum(raw_query * raw_query, axis=1), jnp.sum(raw_k...  13.8 us
    pallas_call x1, Pallas kernels, attend(): pl.pallas_call(functools.partial(attend_kernel, scale=scale, tile=rows //...  13.3 us
    ppermute x1, waiting for transfers between devices, local_split(): shifted = lax.ppermute(tails[1], ('zh', 'y'), [(0, 1), (1, 2), (2, 3)])  6.44 us
  transfers between devices with their start and end apart: 2, of which 2 were waited for; matrix products, arithmetic and copies ran while one was open for 1% of the time, Pallas kernels for 0%

profile of v2, /device:TPU:0, one launch (start us, length us, event | category | flops | bytes accessed | tf_op | source)
XLA Modules:
  0.0 274.2 jit_solution(141235410293733617)
XLA Ops:
  0.0 0.0 copy-start
  0.0 0.0 copy-start.10
  0.0 0.0 copy-start.9
  0.0 1.3 slice.33
  2.6 0.0 copy-start.2
  2.6 0.0 copy-start.3
  2.6 0.0 copy-start.4
  2.6 0.0 copy-start.5
  2.6 0.0 copy-start.6
  2.6 1.7 convert_reduce_fusion
  4.4 1.8 fusion.2
  6.2 0.0 copy-done.10
  6.2 0.1 sine_multiply_fusion
  6.3 0.0 copy-done.9
  6.3 2.0 fusion.6.m_ref
  8.3 0.0 copy-done.2
  8.3 0.0 copy-done.3
  8.3 0.0 copy-done.4
  8.3 0.0 copy-done.5
  8.3 0.0 copy-done.6
  8.4 174.0 %shard_map.127 = (bf16[16,320,1152]{2,1,0:T(8,128)(2,1)}, bf16[8,128,5120]{2,1,0:T(8,128)(2,1)S(1)}, bf16[256,768]{1,0:T(8,128)(2,1)S(1)}) custom-call(bf16[320,1536]{1,0:T(8,128)(2,1)S(1)} %copy-done.2, bf16[320,1536]{1,0:T(8,128)(2,1)S(1)} %copy-done.3, bf16[320,1536]{1,0:T(8,128)(2,1)S(1)} %copy-done.4, bf16[128,5120]{1,0:T(8,128)(2,1)S(1)} %fusion.6.m_ref, ...), custom_call_target="tpu_custom_call" | custom-call | bytes 400000000 | tf_op jit(solution)/shard_map/pallas_call | solution.py:316
  182.4 0.0 copy-start.1
  182.4 20.9 %fusion.19 = (bf16[1024,1152]{1,0:T(8,128)(2,1)S(1)}, f32[1024,1152]{1,0:T(8,128)S(1)}) fusion(bf16[1024,5120]{1,0:T(8,128)(2,1)S(1)} %bitcast.17, bf16[5120,1152]{1,0:T(8,128)(2,1)} %bitcast.25), kind=kOutput, calls=%fused_computation.47 | convolution fusion | flops 12080775168 | bytes 29360128 | tf_op jit(solution)/shard_map/dot_general | solution.py:416
  203.3 0.0 copy-done.1
  203.3 0.0 copy-start.8
  203.3 2.1 copy-done.8
  205.4 0.3 multiply_reduce_fusion.1
  205.8 13.8 %psum.7 = f32[2,1024]{1,0:T(2,128)S(1)} all-reduce(f32[2,1024]{1,0:T(2,128)S(1)} %pad_maximum_fusion.3), channel_id=1, replica_groups=mesh['zh'=2,'zl'=2,'y'=2,'c'=2,'x'=2] {'zl','c','x'}, use_global_device_ids=true, to_apply=%region_4.0 | all-reduce | flops 2048 | bytes 16384 | tf_op jit(solution)/shard_map/psum | solution.py:420
  219.6 0.8 dynamic_slice.10
  220.4 0.8 dynamic_slice.11
  221.1 3.1 %multiply_convert_fusion = (bf16[1024,384]{1,0:T(8,128)(2,1)S(1)}, bf16[1024,384]{1,0:T(8,128)(2,1)}) fusion(f32[1024,1152]{1,0:T(8,128)} %copy-done.8, f32[384]{0:T(512)S(1)} %dynamic_slice.11, f32[1024]{0:T(1024)S(1)} %bitcast.23, f32[384]{0:T(512)S(1)} %dynamic_slice.10, f32[1024]{0:T(1024)S(1)} %bitcast.24), kind=kLoop, calls=%fused_computation.9 | loop fusion | flops 2359296 | bytes 4729856 | tf_op jit(solution)/shard_map/convert_element_type | solution.py:40
  224.3 0.0 copy-start.7
  224.4 0.6 collective-permute-start.1
  225.0 0.8 pad_maximum_fusion.1
  225.7 4.2 %collective-permute-start = (bf16[256,768]{1,0:T(8,128)(2,1)}, bf16[256,768]{1,0:T(8,128)(2,1)}, u32[]{:S(2)}, u32[]{:S(2)}) collective-permute-start(bf16[256,768]{1,0:T(8,128)(2,1)} %pad_maximum_fusion.1), channel_id=1, source_target_pairs={{0,4},{4,16},{16,20},{1,5},{5,17},{17,21},{2,6},{6,18},{18,22},{3,... | collective-permute-start | bytes 1179656 | tf_op jit(solution)/shard_map/ppermute | solution.py:433
  229.9 1.0 slice.47.v_ref.vp_ref
  230.9 0.0 copy-done
  230.9 0.1 constant_dynamic-slice_fusion
  231.0 0.1 copy.14
  231.1 0.1 broadcast_and_fusion
  231.2 0.6 select_n.51.mask_ref
  231.8 3.8 %collective-permute-done.1 = bf16[256,768]{1,0:T(8,128)(2,1)} collective-permute-done((bf16[256,768]{1,0:T(8,128)(2,1)S(1)}, bf16[256,768]{1,0:T(8,128)(2,1)}, u32[]{:S(2)}, u32[]{:S(2)}) %collective-permute-start.1) | collective-permute-done | bytes 393248 | tf_op jit(solution)/shard_map/ppermute | solution.py:432
  235.6 6.4 %collective-permute-done = bf16[256,768]{1,0:T(8,128)(2,1)} collective-permute-done((bf16[256,768]{1,0:T(8,128)(2,1)}, bf16[256,768]{1,0:T(8,128)(2,1)}, u32[]{:S(2)}, u32[]{:S(2)}) %collective-permute-start) | collective-permute-done | bytes 393248 | tf_op jit(solution)/shard_map/ppermute | solution.py:433
  242.1 1.2 broadcast_select_fusion.1
  243.2 0.0 copy-done.7
  243.2 0.9 pad_maximum_fusion.ke_ref.ve_ref
  244.2 13.3 %shard_map.128 = bf16[1024,384]{1,0:T(8,128)(2,1)} custom-call(s32[144]{0:T(256)} %select_n.51.mask_ref, bf16[1024,384]{1,0:T(8,128)(2,1)} %get-tuple-element.14.q_ref, bf16[1024,384]{1,0:T(8,128)(2,1)} %copy-done.7, bf16[1024,384]{1,0:T(8,128)(2,1)} %slice.47.v_ref.vp_ref, bf16[1024,384]{1,0:T(8,128)(2,1)} %copy-done.7, ...), custom_call_target="tpu_custom_call" | custom-call | tf_op jit(solution)/shard_map/pallas_call | solution.py:381
  257.5 15.1 %all_to_all.15 = bf16[4,256,384]{2,1,0:T(8,128)(2,1)S(1)} all-to-all(bf16[4,256,384]{2,1,0:T(8,128)(2,1)} %bitcast.20), channel_id=1, replica_groups=mesh['zh'=2,'zl'=2,'y'=2,'c'=2,'x'=2] {'zl','c'}, dimensions={0} | all-to-all | bytes 1572864 | tf_op jit(solution)/shard_map/all_to_all | solution.py:461
  272.6 0.6 copy.15
  273.2 1.0 copy.16
  (11 shorter events, 0.2 us)
Async XLA Ops:
  0.0 230.9 %copy-start = (s32[12,2,6]{0,1,2:T(2,128)S(1)}, s32[12,2,6]{0,1,2:T(2,128)}, u32[]{:S(2)}) copy-start(s32[12,2,6]{0,1,2:T(2,128)} %param.25) | copy-start | bytes 1732
  0.0 6.2 %copy-start.10 = (f32[5120]{0:T(1024)S(1)}, f32[5120]{0:T(1024)}, u32[]{:S(2)}) copy-start(f32[5120]{0:T(1024)} %param.16) | copy-start | bytes 61444
  0.0 6.3 %copy-start.9 = (f32[5120]{0:T(1024)S(1)}, f32[5120]{0:T(1024)}, u32[]{:S(2)}) copy-start(f32[5120]{0:T(1024)} %param.15) | copy-start | bytes 61444
  2.6 5.7 %copy-start.2 = (bf16[320,1536]{1,0:T(8,128)(2,1)S(1)}, bf16[320,1536]{1,0:T(8,128)(2,1)}, u32[]{:S(2)}) copy-start(bf16[320,1536]{1,0:T(8,128)(2,1)} %wq_ref.1) | copy-start | bytes 2949124
  2.6 5.7 %copy-start.3 = (bf16[320,1536]{1,0:T(8,128)(2,1)S(1)}, bf16[320,1536]{1,0:T(8,128)(2,1)}, u32[]{:S(2)}) copy-start(bf16[320,1536]{1,0:T(8,128)(2,1)} %wk_ref.1) | copy-start | bytes 2949124
  2.6 5.7 %copy-start.4 = (bf16[320,1536]{1,0:T(8,128)(2,1)S(1)}, bf16[320,1536]{1,0:T(8,128)(2,1)}, u32[]{:S(2)}) copy-start(bf16[320,1536]{1,0:T(8,128)(2,1)} %wv_ref.1) | copy-start | bytes 2949124
  2.6 5.7 %copy-start.5 = (bf16[256,1536]{1,0:T(8,128)(2,1)S(1)}, bf16[256,1536]{1,0:T(8,128)(2,1)}, u32[]{:S(2)}) copy-start(bf16[256,1536]{1,0:T(8,128)(2,1)} %ck_ref.1) | copy-start | bytes 2359300
  2.6 5.7 %copy-start.6 = (bf16[256,1536]{1,0:T(8,128)(2,1)S(1)}, bf16[256,1536]{1,0:T(8,128)(2,1)}, u32[]{:S(2)}) copy-start(bf16[256,1536]{1,0:T(8,128)(2,1)} %cv_ref.1) | copy-start | bytes 2359300
  182.4 20.9 %copy-start.1 = (bf16[256,768]{1,0:T(8,128)(2,1)}, bf16[256,768]{1,0:T(8,128)(2,1)S(1)}, u32[]{:S(2)}) copy-start(bf16[256,768]{1,0:T(8,128)(2,1)S(1)} %get-tuple-element.10.kc_ref.vc_ref) | copy-start | bytes 1179652
  203.3 2.1 copy-start.8
  224.3 19.0 %copy-start.7 = (bf16[1024,384]{1,0:T(8,128)(2,1)}, bf16[1024,384]{1,0:T(8,128)(2,1)S(1)}, u32[]{:S(2)}) copy-start(bf16[1024,384]{1,0:T(8,128)(2,1)S(1)} %get-tuple-element.13.k_ref.kp_ref) | copy-start | bytes 2359300
  224.4 11.2 %collective-permute-start.1 = (bf16[256,768]{1,0:T(8,128)(2,1)S(1)}, bf16[256,768]{1,0:T(8,128)(2,1)}, u32[]{:S(2)}, u32[]{:S(2)}) collective-permute-start(bf16[256,768]{1,0:T(8,128)(2,1)S(1)} %pad_maximum_fusion.2), channel_id=1, source_target_pairs={{0,4},{4,0},{1,5},{5,1},{2,6},{6,2},{3,7},{7,3},{8,12},{12,8},{9,1... | collective-permute-start | bytes 1179656 | tf_op jit(solution)/shard_map/ppermute | solution.py:432
  225.7 16.3 %collective-permute-start = (bf16[256,768]{1,0:T(8,128)(2,1)}, bf16[256,768]{1,0:T(8,128)(2,1)}, u32[]{:S(2)}, u32[]{:S(2)}) collective-permute-start(bf16[256,768]{1,0:T(8,128)(2,1)} %pad_maximum_fusion.1), channel_id=1, source_target_pairs={{0,4},{4,16},{16,20},{1,5},{5,17},{17,21},{2,6},{6,18},{18,22},{3,... | collective-permute-start | bytes 1179656 | tf_op jit(solution)/shard_map/ppermute | solution.py:433

commit v3 on v2

--- a/solution.py
+++ b/solution.py
@@ -348,43 +348,195 @@
     return gw.reshape(16 * rows, 3 * half // 4), ga.reshape(8 * tokens, width), cached
 
 
-def attend_kernel(
-    mask_ref, q_ref, k_ref, v_ref, kp_ref, vp_ref, ke_ref, ve_ref, kc_ref, vc_ref, o_ref, *, scale, tile, qtiles, ktiles
+def tail_kernel(
+    raw_ref, qg_ref, kg_ref, bias_ref, cache_ref, o_ref,
+    q_s, k_all, v_all, att, sq, rx, qs, qr, es, er, os_, or_, *, scale, heads, width
 ):
-    g, h = pl.program_id(0), pl.program_id(1)
-    own = g % 2 == 1
-    k_prev = jnp.where(own, kp_ref[...], ke_ref[...])
-    v_prev = jnp.where(own, vp_ref[...], ve_ref[...])
-    keys = jnp.concatenate([kc_ref[...], k_prev, k_ref[...]], axis=0)
-    vals = jnp.concatenate([vc_ref[...], v_prev, v_ref[...]], axis=0)
-    for i in range(qtiles):
-        q = q_ref[i * tile : (i + 1) * tile, :]
-        s = lax.dot_general(q, keys, (((1,), (1,)), ((), ())), preferred_element_type=jnp.float32) * scale
-        parts = []
-        for j in range(ktiles):
-            seen = mask_ref[((g * pl.num_programs(1) + h) * qtiles + i) * ktiles + j]
-            parts.append(jnp.where(seen > 0, s[:, j * tile : (j + 1) * tile], -jnp.inf))
-        s = jnp.concatenate(parts, axis=1)
-        peak = jnp.max(s, axis=-1, keepdims=True)
-        w = jnp.exp(s - peak)
-        total = jnp.sum(w, axis=-1, keepdims=True)
-        summed = jnp.dot(w.astype(jnp.bfloat16), vals, preferred_element_type=jnp.float32)
-        o_ref[i * tile : (i + 1) * tile, :] = (summed / total).astype(jnp.bfloat16)
-
-
-def attend(mask, q, k, v, edges, cached, scale, rows, head, qtiles, ktiles):
-    groups, heads = q.shape[0] // rows, q.shape[1] // head
-    cur = pl.BlockSpec((rows, head), lambda g, h: (g, h))
-    prev = pl.BlockSpec((rows, head), lambda g, h: (jnp.maximum(g - 1, 0), h))
-    edge = [pl.BlockSpec((rows, head), lambda g, h, t=t: (g // 2, t * heads + h)) for t in range(2)]
-    cache = [pl.BlockSpec((rows, head), lambda g, h, t=t: (0, t * heads + h)) for t in range(2)]
+    zh, zl, y, c, x = (lax.axis_index(a) for a in AXES)
+    rows, cols = att.shape[1:]
+    head = cols // heads
+    tile = rows // 2
+    y_here, y_there = (zh, zl, 1 - y, c, x), (1 - zh, zl, 1 - y, c, x)
+
+    def flipped(f):
+        return (zh, 1 - zl if f & 4 else zl, y, 1 - c if f & 2 else c, 1 - x if f & 1 else x)
+
+    barrier = pltpu.get_barrier_semaphore()
+    partners = [flipped(f) for f in range(1, 8)] + [y_here, y_there]
+    for partner in partners:
+        pl.semaphore_signal(barrier, inc=1, device_id=partner, device_id_type=MESH)
+
+    for s in range(4):
+        part = slice(s * rows, (s + 1) * rows)
+        a, b = raw_ref[part, :cols], raw_ref[part, cols : 2 * cols]
+        lanes = lax.broadcasted_iota(jnp.int32, (rows, 128), 1)
+        both = jnp.where(
+            lanes % 8 < 4,
+            jnp.sum(a * a, axis=1, keepdims=True),
+            jnp.sum(b * b, axis=1, keepdims=True),
+        )
+        sq[:, part] = both.T[:8]
+    for s in range(4):
+        v_all[s // 2 * 3 + 1 + s % 2] = raw_ref[s * rows : (s + 1) * rows, 2 * cols :].astype(jnp.bfloat16)
+    pl.semaphore_wait(barrier, len(partners))
+
+    copies = []
+    for f in range(1, 8):
+        cp = pltpu.make_async_remote_copy(
+            src_ref=sq,
+            dst_ref=rx.at[f],
+            send_sem=qs.at[f],
+            recv_sem=qr.at[f],
+            device_id=flipped(f),
+            device_id_type=MESH,
+        )
+        cp.start()
+        copies.append(cp)
+
+    onward = (zh + y - 2 * zh * y, zl, 1 - y, c, x)
+
+    def start_edges(k, ref):
+        out = []
+        for t, (src, dst, target) in enumerate(((2, y, y_here), (5, 1 - y, onward))):
+            cp = pltpu.make_async_remote_copy(
+                src_ref=ref.at[src],
+                dst_ref=ref.at[dst * 3],
+                send_sem=es.at[k, t],
+                recv_sem=er.at[k, t],
+                device_id=target,
+                device_id_type=MESH,
+            )
+            cp.start()
+            out.append(cp)
+        return out
+
+    edges = start_edges(0, v_all)
+    total = sq[...]
+    for f in range(1, 8):
+        copies[f - 1].wait_recv()
+        total = total + rx[f]
+    for s in range(4):
+        part = slice(s * rows, (s + 1) * rows)
+        sums = jnp.concatenate([total[:, part]] * 16, axis=0).T
+        inverse = lax.rsqrt(sums / width + EPSILON)
+        k_all[s // 2 * 3 + 1 + s % 2] = (
+            raw_ref[part, cols : 2 * cols] * inverse[:, 4:5] * kg_ref[...]
+        ).astype(jnp.bfloat16)
+        q_s[s] = (raw_ref[part, :cols] * inverse[:, 0:1] * qg_ref[...]).astype(jnp.bfloat16)
+    edges += start_edges(1, k_all)
+
+    def attend(n, b, d):
+        slot = b * 2 + d
+
+        def one_head(h, carry):
+            span = pl.ds(pl.multiple_of(h * head, head), head)
+            behind = pl.ds(pl.multiple_of(cols + h * head, head), head)
+            old_keys, old_values = cache_ref[:, span], cache_ref[:, behind]
+            near_keys = k_all[pl.ds(b * 3 + d, 2), :, span].reshape(2 * rows, head)
+            near_values = v_all[pl.ds(b * 3 + d, 2), :, span].reshape(2 * rows, head)
+            keys = jnp.concatenate([old_keys, near_keys], axis=0)
+            values = jnp.concatenate([old_values, near_values], axis=0)
+            query = q_s[slot, :, span]
+            for i in range(2):
+                scores = lax.dot_general(
+                    query[i * tile : (i + 1) * tile],
+                    keys,
+                    (((1,), (1,)), ((), ())),
+                    preferred_element_type=jnp.float32,
+                )
+                scores = scores * scale + bias_ref[(slot * heads + h) * 2 + i]
+                peak = jnp.max(scores, axis=-1, keepdims=True)
+                weights = jnp.exp(scores - peak)
+                summed = jnp.dot(weights.astype(jnp.bfloat16), values, preferred_element_type=jnp.float32)
+                att[n, i * tile : (i + 1) * tile, span] = (
+                    summed / jnp.sum(weights, axis=-1, keepdims=True)
+                ).astype(jnp.bfloat16)
+            return carry
+
+        lax.fori_loop(0, heads, one_head, 0)
+
+    me = zl * 2 + c
+
+    def block(p):
+        return o_ref.at[:, pl.ds(pl.multiple_of(p * cols, 128), cols)]
+
+    def push(n, b, d):
+        return pltpu.make_async_remote_copy(
+            src_ref=att.at[n],
+            dst_ref=block(me),
+            send_sem=os_.at[n],
+            recv_sem=or_.at[me],
+            device_id=(zh, b, y, d, x),
+            device_id_type=MESH,
+        )
+
+    order = [(0, 1 - zl, 1), (1, zl, 1), (2, 1 - zl, 0), (3, zl, 0)]
+    for n, b, d in order:
+        if n == 2:
+            for cp in edges:
+                cp.wait_recv()
+        attend(n, b, d)
+        if n % 2 == 0:
+            push(n, b, d).start()
+        else:
+
+            @pl.when(c == d)
+            def _():
+                o_ref[:, pl.ds(pl.multiple_of(me * cols, 128), cols)] = att[n]
+
+            @pl.when(c != d)
+            def _():
+                push(n, b, d).start()
+
+    for p in ((1 - zl) * 2 + c, zl * 2 + 1 - c, (1 - zl) * 2 + 1 - c):
+        pltpu.make_async_remote_copy(
+            src_ref=att.at[0],
+            dst_ref=block(p),
+            send_sem=os_.at[0],
+            recv_sem=or_.at[p],
+            device_id=flipped(4),
+            device_id_type=MESH,
+        ).wait_recv()
+    for cp in copies + edges:
+        cp.wait_send()
+    for n, b, d in order:
+        if n % 2 == 0:
+            push(n, b, d).wait_send()
+        else:
+
+            @pl.when(c != d)
+            def _():
+                push(n, b, d).wait_send()
+
+
+def attend_groups(raw, q_gain, k_gain, bias, cached, scale, heads, width):
+    rows, cols = raw.shape[0] // 4, raw.shape[1] // 3
+    dma = pltpu.SemaphoreType.DMA
+    bf16 = jnp.bfloat16
+    vmem = pl.BlockSpec(memory_space=pltpu.VMEM)
     return pl.pallas_call(
-        functools.partial(attend_kernel, scale=scale, tile=rows // qtiles, qtiles=qtiles, ktiles=ktiles),
-        grid=(groups, heads),
-        out_shape=jax.ShapeDtypeStruct(q.shape, jnp.bfloat16),
-        in_specs=[pl.BlockSpec(memory_space=pltpu.SMEM), cur, cur, cur, prev, prev, *edge, *cache],
-        out_specs=cur,
-    )(mask, q, k, v, k, v, edges, edges, cached, cached)
+        functools.partial(tail_kernel, scale=scale, heads=heads, width=width),
+        out_shape=jax.ShapeDtypeStruct((rows, 4 * cols), bf16),
+        in_specs=[vmem] * 5,
+        out_specs=vmem,
+        scratch_shapes=[
+            pltpu.VMEM((4, rows, cols), bf16),
+            pltpu.VMEM((6, rows, cols), bf16),
+            pltpu.VMEM((6, rows, cols), bf16),
+            pltpu.VMEM((4, rows, cols), bf16),
+            pltpu.VMEM((8, 4 * rows), jnp.float32),
+            pltpu.VMEM((8, 8, 4 * rows), jnp.float32),
+            dma((8,)),
+            dma((8,)),
+            dma((2, 2)),
+            dma((2, 2)),
+            dma((4,)),
+            dma((4,)),
+        ],
+        compiler_params=pltpu.CompilerParams(
+            collective_id=1, has_side_effects=True, vmem_limit_bytes=40 * 1024 * 1024
+        ),
+    )(raw, q_gain, k_gain, bias, cached)
 
 
 def local_split(
@@ -414,26 +566,8 @@
     )
     slab = (zl * 2 + c) * cols
     projected = jnp.dot(tokens, joined, preferred_element_type=jnp.float32)
-    raw_query = projected[:, :cols]
-    raw_key = projected[:, cols : 2 * cols]
-    raw_value = projected[:, 2 * cols :]
-    squares = lax.psum(
-        jnp.stack([jnp.sum(raw_query * raw_query, axis=1), jnp.sum(raw_key * raw_key, axis=1)]),
-        ("zl", "c", "x"),
-    )
-    width = 2 * half
-    q_gain = lax.dynamic_slice_in_dim(query_gain, slab, cols, 0)
-    k_gain = lax.dynamic_slice_in_dim(key_gain, slab, cols, 0)
-    query_rows = scaled_rows(raw_query, squares[0], width, q_gain)
-    key_rows = scaled_rows(raw_key, squares[1], width, k_gain)
-    value_rows = raw_value.astype(jnp.bfloat16)
-    rows = query_rows.shape[0] // 4
-    tails = [jnp.concatenate([a[s * rows : (s + 1) * rows] for a in (key_rows, value_rows)], axis=1) for s in (1, 3)]
-    swapped = lax.ppermute(tails[0], "y", [(0, 1), (1, 0)])
-    shifted = lax.ppermute(tails[1], ("zh", "y"), [(0, 1), (1, 2), (2, 3)])
-    edges = jnp.concatenate(
-        [jnp.where(y == 0, shifted, swapped), jnp.where(y == 0, swapped, shifted)], axis=0
-    )
+    q_gain = lax.dynamic_slice_in_dim(query_gain, slab, cols, 0)[None]
+    k_gain = lax.dynamic_slice_in_dim(key_gain, slab, cols, 0)[None]
     heads = tile_mask.shape[0] // 4
     query_tiles, key_tiles = tile_mask.shape[1:]
     head = cols // heads
@@ -444,22 +578,10 @@
     earlier = (tile_ids >= query_tiles) & (tile_ids < 2 * query_tiles)
     allowed = jnp.where(
         (group_ids == 0)[:, None, None, None] & earlier[None, None, None, :], 0, mask[None]
-    ).reshape(-1)
-    attended = attend(
-        allowed,
-        query_rows,
-        key_rows,
-        value_rows,
-        edges,
-        cached,
-        1.0 / math.sqrt(head),
-        rows,
-        head,
-        query_tiles,
-        key_tiles,
     )
-    out = lax.all_to_all(attended.reshape(4, rows, cols), ("zl", "c"), split_axis=0, concat_axis=2, tiled=True)
-    return out.reshape(rows, half)
+    bias = jnp.repeat(jnp.where(allowed > 0, 0.0, -jnp.inf), latents.shape[0], axis=-1)
+    bias = bias.reshape(4 * heads * query_tiles, 1, -1).astype(jnp.float32)
+    return attend_groups(projected, q_gain, k_gain, bias, cached, 1.0 / math.sqrt(head), heads, 2 * half)
 
 
 def solution(mesh):

time: 277 us -> 235 us (0.85)
  blocking collectives: 28.9 us -> 0 us
  Pallas kernels: 187 us -> 203 us
  waiting for transfers between devices: 10.2 us -> 0 us
  other arithmetic: 12.1 us -> 6.47 us
  starting transfers between devices: 4.75 us -> 0 us
  matrix products: 20.9 us -> 17.1 us
    pallas_call x1, Pallas kernels: 13.3 us -> 28.8 us  [attend_groups(): pl.pallas_call(functools.partial(tail_kernel, scale=scale, heads=heads, w...]
    all_to_all x1 -> x0, blocking collectives: 15.1 us -> none  [local_split(): lax.all_to_all(attended.reshape(4, rows, cols), ('zl', 'c'), split_axis=0...]
    psum x1 -> x0, blocking collectives: 13.8 us -> none  [local_split(): lax.psum(jnp.stack([jnp.sum(raw_query * raw_query, axis=1), jnp.sum(raw_k...]
    ppermute x2 -> x0, waiting for transfers between devices: 10.2 us -> none  [the longest x1 6.44 us: local_split(): shifted = lax.ppermute(tails[1], ('zh', 'y'), [(0, 1), (1, 2), (2, 3)])]
    ppermute x2 -> x0, starting transfers between devices: 4.75 us -> none  [the longest x1 4.2 us: local_split(): shifted = lax.ppermute(tails[1], ('zh', 'y'), [(0, 1), (1, 2), (2, 3)])]
    dot_general x1, matrix products: 20.9 us -> 17.1 us  [local_split(): projected = jnp.dot(tokens, joined, preferred_element_type=jnp.float32)]
    convert_element_type x1 -> x0, other arithmetic: 3.11 us -> none  [scaled_rows(): (raw * lax.rsqrt(squares / width + EPSILON)[:, None] * gain).astype(jnp.b...]
  transfers between devices with their start and end apart: 2 -> 0, of which waited for: 2 -> 0; matrix products, arithmetic and copies ran while one was open for 1% -> 0% of each run, Pallas kernels for 0% -> 0%
where the time goes in v3:
time: 235 us; the launch traced here: 234 us
  Pallas kernels  203 us (86%)
  matrix products  17.1 us (7%)
  other arithmetic  6.47 us (3%)
  local copies, waits for them, and re-layouts  6.41 us (3%)
    pallas_call x1, Pallas kernels, gather_operands(): pl.pallas_call(gather_kernel, out_shape=(jax.ShapeDtypeStruct((16, rows,...  174 us
    pallas_call x1, Pallas kernels, attend_groups(): pl.pallas_call(functools.partial(tail_kernel, scale=scale, heads=heads, w...  28.8 us
    dot_general x1, matrix products, local_split(): projected = jnp.dot(tokens, joined, preferred_element_type=jnp.float32)  17.1 us

profile of v3, /device:TPU:0, one launch (start us, length us, event | category | flops | bytes accessed | tf_op | source)
XLA Modules:
  0.0 234.3 jit_solution(9002017674002699151)
XLA Ops:
  0.0 0.0 copy-start
  0.0 0.0 copy-start.7
  0.0 1.3 slice.3
  2.6 0.8 sine_multiply_fusion
  3.4 0.0 copy-start.2
  3.4 0.0 copy-start.3
  3.4 0.0 copy-start.4
  3.5 0.0 copy-start.5
  3.5 0.0 copy-start.6
  3.5 1.7 convert_reduce_fusion
  5.2 1.8 fusion.2
  7.0 0.0 copy-done.7
  7.1 2.0 fusion.6.m_ref
  9.0 0.0 copy-done.2
  9.0 0.0 copy-done.3
  9.0 0.0 copy-done.4
  9.0 0.0 copy-done.5
  9.1 0.0 copy-done.6
  9.1 174.0 %shard_map.127 = (bf16[16,320,1152]{2,1,0:T(8,128)(2,1)}, bf16[8,128,5120]{2,1,0:T(8,128)(2,1)S(1)}, bf16[256,768]{1,0:T(8,128)(2,1)S(1)}) custom-call(bf16[320,1536]{1,0:T(8,128)(2,1)S(1)} %copy-done.2, bf16[320,1536]{1,0:T(8,128)(2,1)S(1)} %copy-done.3, bf16[320,1536]{1,0:T(8,128)(2,1)S(1)} %copy-done.4, bf16[128,5120]{1,0:T(8,128)(2,1)S(1)} %fusion.6.m_ref, ...), custom_call_target="tpu_custom_call" | custom-call | bytes 400000000 | tf_op jit(solution)/shard_map/pallas_call | solution.py:316
  183.1 17.1 %fusion.13.raw_ref = f32[1024,1152]{1,0:T(8,128)} fusion(bf16[1024,5120]{1,0:T(8,128)(2,1)S(1)} %bitcast.6, bf16[5120,1152]{1,0:T(8,128)(2,1)} %bitcast.7), kind=kOutput, calls=%fused_computation.29 | convolution fusion | flops 12079595520 | bytes 27000832 | tf_op jit(solution)/shard_map/dot_general | solution.py:568
  200.2 0.0 copy-done
  200.2 0.1 constant_dynamic-slice_fusion
  200.3 0.1 copy.15
  200.4 0.1 broadcast_and_fusion
  200.5 0.1 broadcast_in_dim.56
  200.6 0.1 reshape_reshape.4.bias_ref
  200.6 0.8 dynamic_slice.9
  201.4 0.8 dynamic_slice.10
  202.2 0.0 copy-start.1
  202.2 2.3 copy-done.1
  204.5 28.8 %shard_map.128 = bf16[256,1536]{1,0:T(8,128)(2,1)S(1)} custom-call(f32[1024,1152]{1,0:T(8,128)S(1)} %copy-done.1, f32[1,384]{1,0:T(1,128)S(1)} %broadcast_in_dim.49.qg_ref, f32[1,384]{1,0:T(1,128)S(1)} %broadcast_in_dim.50.kg_ref, f32[24,1,768]{2,1,0:T(1,128)S(1)} %reshape_reshape.4.bias_ref, bf16[256,768]{1,0:T(8,128)(2,1)S(1)} %get-tuple-element.10.cache_ref), custom_call_target="tpu_custom_call" | custom-call | tf_op jit(solution)/shard_map/pallas_call | solution.py:517
  233.4 0.9 copy.19
  (8 shorter events, 0.1 us)
Async XLA Ops:
  0.0 200.2 %copy-start = (s32[12,2,6]{0,1,2:T(2,128)S(1)}, s32[12,2,6]{0,1,2:T(2,128)}, u32[]{:S(2)}) copy-start(s32[12,2,6]{0,1,2:T(2,128)} %param.25) | copy-start | bytes 1732
  0.0 7.0 %copy-start.7 = (f32[5120]{0:T(1024)S(1)}, f32[5120]{0:T(1024)}, u32[]{:S(2)}) copy-start(f32[5120]{0:T(1024)} %param.15) | copy-start | bytes 61444
  3.4 5.6 %copy-start.2 = (bf16[320,1536]{1,0:T(8,128)(2,1)S(1)}, bf16[320,1536]{1,0:T(8,128)(2,1)}, u32[]{:S(2)}) copy-start(bf16[320,1536]{1,0:T(8,128)(2,1)} %wq_ref.1) | copy-start | bytes 2949124
  3.4 5.6 %copy-start.3 = (bf16[320,1536]{1,0:T(8,128)(2,1)S(1)}, bf16[320,1536]{1,0:T(8,128)(2,1)}, u32[]{:S(2)}) copy-start(bf16[320,1536]{1,0:T(8,128)(2,1)} %wk_ref.1) | copy-start | bytes 2949124
  3.4 5.6 %copy-start.4 = (bf16[320,1536]{1,0:T(8,128)(2,1)S(1)}, bf16[320,1536]{1,0:T(8,128)(2,1)}, u32[]{:S(2)}) copy-start(bf16[320,1536]{1,0:T(8,128)(2,1)} %wv_ref.1) | copy-start | bytes 2949124
  3.5 5.6 %copy-start.5 = (bf16[256,1536]{1,0:T(8,128)(2,1)S(1)}, bf16[256,1536]{1,0:T(8,128)(2,1)}, u32[]{:S(2)}) copy-start(bf16[256,1536]{1,0:T(8,128)(2,1)} %ck_ref.1) | copy-start | bytes 2359300
  3.5 5.6 %copy-start.6 = (bf16[256,1536]{1,0:T(8,128)(2,1)S(1)}, bf16[256,1536]{1,0:T(8,128)(2,1)}, u32[]{:S(2)}) copy-start(bf16[256,1536]{1,0:T(8,128)(2,1)} %cv_ref.1) | copy-start | bytes 2359300
  202.2 2.3 copy-start.1

commit v4 on v3

--- a/solution.py
+++ b/solution.py
@@ -141,8 +141,8 @@
 
 
 def gather_kernel(
-    wq_ref, wk_ref, wv_ref, m_ref, ck_ref, cv_ref, flag_ref, gw_ref, ga_ref, cache_ref,
-    kept, from_c, halves, from_z, part, from_y, from_zh, ws, wr, ys, yr, as_, ar, ls, cs, cr
+    wq_ref, wk_ref, wv_ref, lat_ref, gain_ref, shift_ref, ck_ref, cv_ref, flag_ref, gw_ref, ga_ref, cache_ref,
+    m_ref,    kept, from_c, halves, from_z, part, from_y, from_zh, ws, wr, ys, yr, as_, ar, ls, cs, cr
 ):
     zh, zl, y, c, x = (lax.axis_index(a) for a in AXES)
     weights = (wq_ref, wk_ref, wv_ref)
@@ -169,43 +169,39 @@
     me = place(zh, zl, y, c)
     wcopies = {}
 
-    def start_weights(f):
+    def start_weights(f, t):
         a, b, d = flipped(f)
         slab = (b * 2 + d) * cols
-        out = []
-        for t in range(3):
-            src = weights[t].at[:, pl.ds(pl.multiple_of(slab, 128), cols)]
-            dst = gw_ref.at[me, :, pl.ds(t * cols, cols)]
-            if f == 0:
-                cp = pltpu.make_async_copy(src, dst, wr.at[f, t])
-            else:
-                cp = pltpu.make_async_remote_copy(
-                    src_ref=src,
-                    dst_ref=dst,
-                    send_sem=ws.at[f, t],
-                    recv_sem=wr.at[f, t],
-                    device_id=(a, b, y, d, x),
-                    device_id_type=MESH,
-                )
-            cp.start()
-            out.append(cp)
-        wcopies[f] = out
+        src = weights[t].at[:, pl.ds(pl.multiple_of(slab, 128), cols)]
+        dst = gw_ref.at[me, :, pl.ds(t * cols, cols)]
+        if f == 0:
+            cp = pltpu.make_async_copy(src, dst, wr.at[f, t])
+        else:
+            cp = pltpu.make_async_remote_copy(
+                src_ref=src,
+                dst_ref=dst,
+                send_sem=ws.at[f, t],
+                recv_sem=wr.at[f, t],
+                device_id=(a, b, y, d, x),
+                device_id_type=MESH,
+            )
+        cp.start()
+        wcopies[f, t] = cp
 
     ycopies = []
 
-    def forward(f):
-        for cp in wcopies[f]:
-            if f == 0:
-                cp.wait()
-            else:
-                cp.wait_recv()
+    def forward(f, t):
+        if f == 0:
+            wcopies[f, t].wait()
+        else:
+            wcopies[f, t].wait_recv()
         a, b, d = flipped(f)
-        slot = place(a, b, y, d)
+        piece = gw_ref.at[place(a, b, y, d), :, pl.ds(t * cols, cols)]
         cp = pltpu.make_async_remote_copy(
-            src_ref=gw_ref.at[slot],
-            dst_ref=gw_ref.at[slot],
-            send_sem=ys.at[f],
-            recv_sem=yr.at[f],
+            src_ref=piece,
+            dst_ref=piece,
+            send_sem=ys.at[f, t],
+            recv_sem=yr.at[f, t],
             device_id=(zh, zl, 1 - y, c, x),
             device_id_type=MESH,
         )
@@ -242,53 +238,76 @@
         return cp
 
     to_z, to_x, to_c = (zh, 1 - zl, y, c, x), (zh, zl, y, c, 1 - x), (zh, zl, y, 1 - c, x)
+    far_pieces = [(f, t) for f in (4, 5, 6, 7) for t in range(3)]
+    window = 4
+    for f in (0, 1):
+        for t in range(3):
+            start_weights(f, t)
+    for piece in far_pieces[:window]:
+        start_weights(*piece)
+    for t in range(3):
+        start_weights(2, t)
+    for t in range(3):
+        forward(0, t)
+
+    def modulate_rows(i, carry):
+        part = pl.ds(pl.multiple_of(i * 16, 16), 16)
+        values = lat_ref[part, :].astype(jnp.float32)
+        centred = values - jnp.mean(values, axis=-1, keepdims=True)
+        spread = jnp.mean(centred * centred, axis=-1, keepdims=True)
+        normed = centred * lax.rsqrt(spread + EPSILON)
+        m_ref[part, :] = (normed * gain_ref[...] + shift_ref[...]).astype(jnp.bfloat16)
+        return carry
+
+    lax.fori_loop(0, lat_ref.shape[0] // 16, modulate_rows, 0)
     mine = token_slot(zl, c, x)
     start_tokens(0, m_ref, mine, to_z)
-    start_weights(0)
-    start_weights(1)
-    start_weights(4)
     start_tokens(1, m_ref, mine, to_x)
     start_tokens(2, m_ref, mine, to_c)
     local = pltpu.make_async_copy(m_ref, ga_ref.at[mine], ls.at[0])
     local.start()
-    start_weights(5)
-    forward(0)
+    for t in range(3):
+        start_weights(3, t)
+    for t in range(3):
+        forward(1, t)
     for p in range(4):
         for t, ref in enumerate((ck_ref, cv_ref)):
             block = ref[:, p * cols : (p + 1) * cols].astype(jnp.float32) * flag_ref[...]
             kept[p, :, t * cols : (t + 1) * cols] = block.astype(jnp.bfloat16)
     cache_c = [start_cache(j, kept.at[2 * j + 1 - c], from_c.at[j], to_c) for j in range(2)]
-    forward(1)
-    for j in range(2):
-        cache_c[j].wait()
-        halves[j] = kept[2 * j + c] + from_c[j]
-    cache_z = start_cache(2, halves.at[1 - zl], from_z, to_z)
-    acopies[0].wait_recv()
-    theirs = token_slot(1 - zl, c, x)
-    start_tokens(3, ga_ref.at[theirs], theirs, to_x)
-    start_tokens(4, ga_ref.at[theirs], theirs, to_c)
-    start_weights(2)
-    forward(4)
-    cache_z.wait()
-    part[0] = halves[zl] + from_z[...]
-    cache_y = start_cache(3, part.at[0], from_y, (zh, zl, 1 - y, c, x))
-    start_weights(6)
-    start_weights(3)
-    acopies[1].wait_recv()
-    across = token_slot(zl, c, 1 - x)
-    start_tokens(5, ga_ref.at[across], across, to_c)
-    forward(2)
-    forward(5)
-    start_weights(7)
-    cache_y.wait()
-    part[1] = part[0] + from_y[...]
-    cache_zh = start_cache(4, part.at[1], from_zh, (1 - zh, zl, y, c, x))
+    for at, piece in enumerate(far_pieces):
+        forward(*piece)
+        if at + window < len(far_pieces):
+            start_weights(*far_pieces[at + window])
+        if at == 0:
+            for j in range(2):
+                cache_c[j].wait()
+                halves[j] = kept[2 * j + c] + from_c[j]
+            cache_z = start_cache(2, halves.at[1 - zl], from_z, to_z)
+        if at in (1, 2, 3):
+            forward(2, at - 1)
+        if at == 3:
+            acopies[0].wait_recv()
+            theirs = token_slot(1 - zl, c, x)
+            start_tokens(3, ga_ref.at[theirs], theirs, to_x)
+            start_tokens(4, ga_ref.at[theirs], theirs, to_c)
+        if at in (4, 5, 6):
+            forward(3, at - 4)
+        if at == 4:
+            cache_z.wait()
+            part[0] = halves[zl] + from_z[...]
+            cache_y = start_cache(3, part.at[0], from_y, (zh, zl, 1 - y, c, x))
+        if at == 6:
+            acopies[1].wait_recv()
+            across = token_slot(zl, c, 1 - x)
+            start_tokens(5, ga_ref.at[across], across, to_c)
+        if at == 8:
+            cache_y.wait()
+            part[1] = part[0] + from_y[...]
+            cache_zh = start_cache(4, part.at[1], from_zh, (1 - zh, zl, y, c, x))
     acopies[3].wait_recv()
     far = token_slot(1 - zl, c, 1 - x)
     start_tokens(6, ga_ref.at[far], far, to_c)
-    forward(3)
-    forward(6)
-    forward(7)
     cache_zh.wait()
     cache_ref[...] = part[1] + from_zh[...]
     local.wait()
@@ -296,8 +315,8 @@
         acopies[k].wait_recv()
     for cp in ycopies:
         cp.wait_recv()
-    for f in range(1, 8):
-        for cp in wcopies[f]:
+    for (f, t), cp in wcopies.items():
+        if f:
             cp.wait_send()
     for cp in ycopies:
         cp.wait_send()
@@ -305,9 +324,9 @@
         acopies[k].wait_send()
 
 
-def gather_operands(w_query, w_key, w_value, modulated, cache_keys, cache_values, flag):
+def gather_operands(w_query, w_key, w_value, latents, gain, shift, cache_keys, cache_values, flag):
     rows, half = w_query.shape
-    tokens, width = modulated.shape
+    tokens, width = latents.shape
     dma = pltpu.SemaphoreType.DMA
     anywhere = pl.BlockSpec(memory_space=pl.ANY)
     vmem = pl.BlockSpec(memory_space=pltpu.VMEM)
@@ -317,12 +336,13 @@
         gather_kernel,
         out_shape=(
             jax.ShapeDtypeStruct((16, rows, 3 * half // 4), w_query.dtype),
-            jax.ShapeDtypeStruct((8, tokens, width), modulated.dtype),
+            jax.ShapeDtypeStruct((8, tokens, width), latents.dtype),
             jax.ShapeDtypeStruct(slab, bf16),
         ),
-        in_specs=[anywhere] * 4 + [vmem] * 3,
+        in_specs=[anywhere] * 3 + [vmem] * 6,
         out_specs=(anywhere, anywhere, vmem),
         scratch_shapes=[
+            pltpu.VMEM((tokens, width), bf16),
             pltpu.VMEM((4, *slab), bf16),
             pltpu.VMEM((2, *slab), bf16),
             pltpu.VMEM((2, *slab), bf16),
@@ -332,8 +352,8 @@
             pltpu.VMEM(slab, bf16),
             dma((8, 3)),
             dma((8, 3)),
-            dma((8,)),
-            dma((8,)),
+            dma((8, 3)),
+            dma((8, 3)),
             dma((7,)),
             dma((7,)),
             dma((1,)),
@@ -344,7 +364,7 @@
             collective_id=0, has_side_effects=True, vmem_limit_bytes=32 * 1024 * 1024
         ),
         cost_estimate=pl.CostEstimate(flops=0, bytes_accessed=400_000_000, transcendentals=0),
-    )(w_query, w_key, w_value, modulated, cache_keys, cache_values, flag)
+    )(w_query, w_key, w_value, latents, gain, shift, cache_keys, cache_values, flag)
     return gw.reshape(16 * rows, 3 * half // 4), ga.reshape(8 * tokens, width), cached
 
 
@@ -556,13 +576,16 @@
 ):
     zh, zl, y, c, x = (lax.axis_index(a) for a in AXES)
     member = ((zh * 2 + zl) * 2 + y) * 2 + c
-    modulated = modulate(latents, timesteps[0], mod_shift, mod_scale)
+    freqs = jnp.exp(-math.log(10000.0) * jnp.arange(latents.shape[1], dtype=jnp.float32) / latents.shape[1])
+    angles = timesteps[0].astype(jnp.float32) * freqs
+    gain = (1.0 + mod_scale + 0.5 * jnp.cos(angles))[None]
+    shift = (mod_shift + 0.5 * jnp.sin(angles))[None]
     root = owners[owners.shape[0] - 1]
     half = w_query.shape[1]
     cols = half // 4
     flag = jnp.full((1, cols), member == root, jnp.float32)
     joined, tokens, cached = gather_operands(
-        w_query, w_key, w_value, modulated, cache_keys, cache_values, flag
+        w_query, w_key, w_value, latents, gain, shift, cache_keys, cache_values, flag
     )
     slab = (zl * 2 + c) * cols
     projected = jnp.dot(tokens, joined, preferred_element_type=jnp.float32)

time: 235 us -> 236 us (level)
  local copies, waits for them, and re-layouts: 6.41 us -> 13.5 us
  other arithmetic: 6.47 us -> 0.96 us
    unnamed x17, local copies, waits for them, and re-layouts: 3.26 us -> 10.4 us
    reduce_sum x2 -> x0, other arithmetic: 3.55 us -> none  [the longest x1 1.82 us: modulate(): spread = jnp.mean(centred * centred, axis=-1, keepdims=True)]
where the time goes in v4:
time: 236 us
  Pallas kernels  203 us (86%)
  matrix products  17.1 us (7%)
  local copies, waits for them, and re-layouts  13.5 us (6%)
    pallas_call x1, Pallas kernels, gather_operands(): pl.pallas_call(gather_kernel, out_shape=(jax.ShapeDtypeStruct((16, rows,...  172 us
    pallas_call x1, Pallas kernels, attend_groups(): pl.pallas_call(functools.partial(tail_kernel, scale=scale, heads=heads, w...  30.3 us
    dot_general x1, matrix products, local_split(): projected = jnp.dot(tokens, joined, preferred_element_type=jnp.float32)  17.1 us
    unnamed x17, local copies, waits for them, and re-layouts  10.4 us

profile of v4, /device:TPU:0, one launch (start us, length us, event | category | flops | bytes accessed | tf_op | source)
XLA Modules:
  0.0 235.6 jit_solution(8245153470134438624)
XLA Ops:
  0.0 0.0 copy-start
  0.7 0.9 multiply_add_fusion
  1.5 1.2 slice.3
  3.4 0.0 copy-start.2
  3.5 1.3 copy-done.2
  4.8 0.0 copy-start.3
  4.8 1.2 copy-done.3
  6.0 0.0 copy-start.4
  6.0 1.2 copy-done.4
  7.2 0.0 copy-start.5
  7.2 1.2 copy-done.5
  8.4 0.0 copy-start.6
  8.4 1.1 copy-done.6
  9.5 0.0 copy-start.7
  9.5 1.1 copy-done.7
  10.6 172.2 %shard_map.127 = (bf16[16,320,1152]{2,1,0:T(8,128)(2,1)}, bf16[8,128,5120]{2,1,0:T(8,128)(2,1)S(1)}, bf16[256,768]{1,0:T(8,128)(2,1)S(1)}) custom-call(bf16[320,1536]{1,0:T(8,128)(2,1)S(1)} %copy-done.3, bf16[320,1536]{1,0:T(8,128)(2,1)S(1)} %copy-done.4, bf16[320,1536]{1,0:T(8,128)(2,1)S(1)} %copy-done.5, bf16[128,5120]{1,0:T(8,128)(2,1)S(1)} %copy-done.2, ...), custom_call_target="tpu_custom_call" | custom-call | bytes 400000000 | tf_op jit(solution)/shard_map/pallas_call | solution.py:335
  182.9 17.1 %fusion.6.raw_ref = f32[1024,1152]{1,0:T(8,128)} fusion(bf16[1024,5120]{1,0:T(8,128)(2,1)S(1)} %bitcast.10, bf16[5120,1152]{1,0:T(8,128)(2,1)} %bitcast.11), kind=kOutput, calls=%fused_computation.18 | convolution fusion | flops 12079595520 | bytes 27000832 | tf_op jit(solution)/shard_map/dot_general | solution.py:591
  200.0 0.8 dynamic_slice.9
  200.8 0.8 dynamic_slice.10
  201.6 0.1 broadcast_and_fusion
  201.7 0.0 copy-done
  201.7 0.1 constant_dynamic-slice_fusion
  201.7 0.1 copy.15
  201.9 0.1 broadcast_in_dim.59
  201.9 0.1 reshape_reshape.4.bias_ref
  202.0 0.0 copy-start.1
  202.0 2.3 copy-done.1
  204.4 30.3 %shard_map.128 = bf16[256,1536]{1,0:T(8,128)(2,1)S(1)} custom-call(f32[1024,1152]{1,0:T(8,128)S(1)} %copy-done.1, f32[1,384]{1,0:T(1,128)S(1)} %broadcast_in_dim.52.qg_ref, f32[1,384]{1,0:T(1,128)S(1)} %broadcast_in_dim.53.kg_ref, f32[24,1,768]{2,1,0:T(1,128)S(1)} %reshape_reshape.4.bias_ref, bf16[256,768]{1,0:T(8,128)(2,1)S(1)} %get-tuple-element.10.cache_ref), custom_call_target="tpu_custom_call" | custom-call | tf_op jit(solution)/shard_map/pallas_call | solution.py:537
  234.7 0.9 copy.19
  (6 shorter events, 0.0 us)
Async XLA Ops:
  0.0 201.7 %copy-start = (s32[12,2,6]{0,1,2:T(2,128)S(1)}, s32[12,2,6]{0,1,2:T(2,128)}, u32[]{:S(2)}) copy-start(s32[12,2,6]{0,1,2:T(2,128)} %param.25) | copy-start | bytes 1732
  3.4 1.3 copy-start.2
  4.8 1.2 copy-start.3
  6.0 1.2 copy-start.4
  7.2 1.2 copy-start.5
  8.4 1.1 copy-start.6
  9.5 1.1 copy-start.7
  202.0 2.3 copy-start.1

commit v5 on v4

--- a/solution.py
+++ b/solution.py
@@ -141,8 +141,8 @@
 
 
 def gather_kernel(
-    wq_ref, wk_ref, wv_ref, lat_ref, gain_ref, shift_ref, ck_ref, cv_ref, flag_ref, gw_ref, ga_ref, cache_ref,
-    m_ref,    kept, from_c, halves, from_z, part, from_y, from_zh, ws, wr, ys, yr, as_, ar, ls, cs, cr
+    wq_ref, wk_ref, wv_ref, lat_hbm, ck_hbm, cv_hbm, gain_ref, shift_ref, flag_ref, gw_ref, ga_ref, cache_ref,
+    m_ref, lat_ref, ck_ref, cv_ref, ins,    kept, from_c, halves, from_z, part, from_y, from_zh, ws, wr, ys, yr, as_, ar, ls, cs, cr
 ):
     zh, zl, y, c, x = (lax.axis_index(a) for a in AXES)
     weights = (wq_ref, wk_ref, wv_ref)
@@ -159,6 +159,11 @@
     def place(fzh, fzl, fy, fc):
         return ((fzh * 2 + fzl) * 2 + fy) * 2 + fc
 
+    loads = []
+    for k, (src, dst) in enumerate(((lat_hbm, lat_ref), (ck_hbm, ck_ref), (cv_hbm, cv_ref))):
+        load = pltpu.make_async_copy(src, dst, ins.at[k])
+        load.start()
+        loads.append(load)
     barrier = pltpu.get_barrier_semaphore()
     partners = [(a, b, y, d, x) for a, b, d in map(flipped, range(1, 8))]
     partners += [(zh, zl, 1 - y, c, x), (zh, zl, y, c, 1 - x)]
@@ -238,6 +243,9 @@
         return cp
 
     to_z, to_x, to_c = (zh, 1 - zl, y, c, x), (zh, zl, y, c, 1 - x), (zh, zl, y, 1 - c, x)
+    few = from_y.shape[0]
+    held = pl.ds(pl.multiple_of(y * few, few), few)
+    sent = pl.ds(pl.multiple_of((1 - y) * few, few), few)
     far_pieces = [(f, t) for f in (4, 5, 6, 7) for t in range(3)]
     window = 4
     for f in (0, 1):
@@ -259,6 +267,7 @@
         m_ref[part, :] = (normed * gain_ref[...] + shift_ref[...]).astype(jnp.bfloat16)
         return carry
 
+    loads[0].wait()
     lax.fori_loop(0, lat_ref.shape[0] // 16, modulate_rows, 0)
     mine = token_slot(zl, c, x)
     start_tokens(0, m_ref, mine, to_z)
@@ -270,6 +279,8 @@
         start_weights(3, t)
     for t in range(3):
         forward(1, t)
+    loads[1].wait()
+    loads[2].wait()
     for p in range(4):
         for t, ref in enumerate((ck_ref, cv_ref)):
             block = ref[:, p * cols : (p + 1) * cols].astype(jnp.float32) * flag_ref[...]
@@ -296,20 +307,24 @@
         if at == 4:
             cache_z.wait()
             part[0] = halves[zl] + from_z[...]
-            cache_y = start_cache(3, part.at[0], from_y, (zh, zl, 1 - y, c, x))
+            cache_y = start_cache(3, part.at[0, sent], from_y, (zh, zl, 1 - y, c, x))
         if at == 6:
             acopies[1].wait_recv()
             across = token_slot(zl, c, 1 - x)
             start_tokens(5, ga_ref.at[across], across, to_c)
-        if at == 8:
+        if at == 6:
             cache_y.wait()
-            part[1] = part[0] + from_y[...]
-            cache_zh = start_cache(4, part.at[1], from_zh, (1 - zh, zl, y, c, x))
+            part[1, held] = part[0, held] + from_y[...]
+            cache_zh = start_cache(4, part.at[1, held], from_zh, (1 - zh, zl, y, c, x))
+        if at == 9:
+            cache_zh.wait()
+            cache_ref[held] = part[1, held] + from_zh[...]
+            half = cache_ref.at[held]
+            cache_last = start_cache(5, half, half, (zh, zl, 1 - y, c, x))
     acopies[3].wait_recv()
     far = token_slot(1 - zl, c, 1 - x)
     start_tokens(6, ga_ref.at[far], far, to_c)
-    cache_zh.wait()
-    cache_ref[...] = part[1] + from_zh[...]
+    cache_last.wait()
     local.wait()
     for k in (2, 4, 5, 6):
         acopies[k].wait_recv()
@@ -324,7 +339,7 @@
         acopies[k].wait_send()
 
 
-def gather_operands(w_query, w_key, w_value, latents, gain, shift, cache_keys, cache_values, flag):
+def gather_operands(w_query, w_key, w_value, latents, cache_keys, cache_values, gain, shift, flag):
     rows, half = w_query.shape
     tokens, width = latents.shape
     dma = pltpu.SemaphoreType.DMA
@@ -339,17 +354,21 @@
             jax.ShapeDtypeStruct((8, tokens, width), latents.dtype),
             jax.ShapeDtypeStruct(slab, bf16),
         ),
-        in_specs=[anywhere] * 3 + [vmem] * 6,
+        in_specs=[anywhere] * 6 + [vmem] * 3,
         out_specs=(anywhere, anywhere, vmem),
         scratch_shapes=[
             pltpu.VMEM((tokens, width), bf16),
+            pltpu.VMEM((tokens, width), bf16),
+            pltpu.VMEM(cache_keys.shape, bf16),
+            pltpu.VMEM(cache_keys.shape, bf16),
+            dma((3,)),
             pltpu.VMEM((4, *slab), bf16),
             pltpu.VMEM((2, *slab), bf16),
             pltpu.VMEM((2, *slab), bf16),
             pltpu.VMEM(slab, bf16),
             pltpu.VMEM((2, *slab), bf16),
-            pltpu.VMEM(slab, bf16),
-            pltpu.VMEM(slab, bf16),
+            pltpu.VMEM((slab[0] // 2, slab[1]), bf16),
+            pltpu.VMEM((slab[0] // 2, slab[1]), bf16),
             dma((8, 3)),
             dma((8, 3)),
             dma((8, 3)),
@@ -357,14 +376,14 @@
             dma((7,)),
             dma((7,)),
             dma((1,)),
-            dma((5,)),
-            dma((5,)),
+            dma((6,)),
+            dma((6,)),
         ],
         compiler_params=pltpu.CompilerParams(
-            collective_id=0, has_side_effects=True, vmem_limit_bytes=32 * 1024 * 1024
+            collective_id=0, has_side_effects=True, vmem_limit_bytes=56 * 1024 * 1024
         ),
         cost_estimate=pl.CostEstimate(flops=0, bytes_accessed=400_000_000, transcendentals=0),
-    )(w_query, w_key, w_value, latents, gain, shift, cache_keys, cache_values, flag)
+    )(w_query, w_key, w_value, latents, cache_keys, cache_values, gain, shift, flag)
     return gw.reshape(16 * rows, 3 * half // 4), ga.reshape(8 * tokens, width), cached
 
 
@@ -554,7 +573,7 @@
             dma((4,)),
         ],
         compiler_params=pltpu.CompilerParams(
-            collective_id=1, has_side_effects=True, vmem_limit_bytes=40 * 1024 * 1024
+            collective_id=1, has_side_effects=True, vmem_limit_bytes=20 * 1024 * 1024
         ),
     )(raw, q_gain, k_gain, bias, cached)
 
@@ -585,7 +604,7 @@
     cols = half // 4
     flag = jnp.full((1, cols), member == root, jnp.float32)
     joined, tokens, cached = gather_operands(
-        w_query, w_key, w_value, latents, gain, shift, cache_keys, cache_values, flag
+        w_query, w_key, w_value, latents, cache_keys, cache_values, gain, shift, flag
     )
     slab = (zl * 2 + c) * cols
     projected = jnp.dot(tokens, joined, preferred_element_type=jnp.float32)

time: 236 us -> 247 us (1.047)
  Pallas kernels: 203 us -> 218 us
  local copies, waits for them, and re-layouts: 13.5 us -> 6.89 us
    pallas_call x1, Pallas kernels: 172 us -> 189 us  [gather_operands(): pl.pallas_call(gather_kernel, out_shape=(jax.ShapeDtypeStruct((16, rows,...]
    unnamed x17 -> x7, local copies, waits for them, and re-layouts: 10.4 us -> 3.22 us
where the time goes in v5:
time: 247 us
  Pallas kernels  218 us (88%)
  matrix products  19.1 us (8%)
  local copies, waits for them, and re-layouts  6.89 us (3%)
    pallas_call x1, Pallas kernels, gather_operands(): pl.pallas_call(gather_kernel, out_shape=(jax.ShapeDtypeStruct((16, rows,...  189 us
    pallas_call x1, Pallas kernels, attend_groups(): pl.pallas_call(functools.partial(tail_kernel, scale=scale, heads=heads, w...  29 us
    dot_general x1, matrix products, local_split(): projected = jnp.dot(tokens, joined, preferred_element_type=jnp.float32)  19.1 us

profile of v5, /device:TPU:0, one launch (start us, length us, event | category | flops | bytes accessed | tf_op | source)
XLA Modules:
  0.0 246.7 jit_solution(15621198159324133460)
XLA Ops:
  0.0 0.0 copy-start
  0.7 1.5 multiply_add_fusion
  2.1 1.2 slice.3
  4.0 0.5 broadcast_in_dim.51.flag_ref
  4.6 188.8 %shard_map.127 = (bf16[16,320,1152]{2,1,0:T(8,128)(2,1)}, bf16[8,128,5120]{2,1,0:T(8,128)(2,1)}, bf16[256,768]{1,0:T(8,128)(2,1)}) custom-call(bf16[320,1536]{1,0:T(8,128)(2,1)} %wq_ref.1, bf16[320,1536]{1,0:T(8,128)(2,1)} %wk_ref.1, bf16[320,1536]{1,0:T(8,128)(2,1)} %wv_ref.1, bf16[128,5120]{1,0:T(8,128)(2,1)} %lat_hbm.1, bf16[256,1536]{1,0:T(8,128)(2,1)} %ck_hbm.1, ...), custom_call_target="tpu_custom_call" | custom-call | bytes 400000000 | tf_op jit(solution)/shard_map/pallas_call | solution.py:350
  193.3 0.0 copy-start.2
  193.3 19.1 %fusion.6.raw_ref = f32[1024,1152]{1,0:T(8,128)} fusion(bf16[1024,5120]{1,0:T(8,128)(2,1)} %bitcast.11, bf16[5120,1152]{1,0:T(8,128)(2,1)} %bitcast.10), kind=kOutput, calls=%fused_computation.18 | convolution fusion | flops 12079595520 | bytes 27000832 | tf_op jit(solution)/shard_map/dot_general | solution.py:610
  212.4 0.8 dynamic_slice.9
  213.2 0.8 dynamic_slice.10
  214.0 0.1 broadcast_and_fusion
  214.1 0.0 copy-done
  214.1 0.1 constant_dynamic-slice_fusion
  214.2 0.1 copy.15
  214.3 0.1 broadcast_in_dim.59
  214.4 0.1 reshape_reshape.4.bias_ref
  214.5 0.0 copy-done.2
  214.5 0.0 copy-start.1
  214.5 2.3 copy-done.1
  216.8 29.0 %shard_map.128 = bf16[256,1536]{1,0:T(8,128)(2,1)S(1)} custom-call(f32[1024,1152]{1,0:T(8,128)S(1)} %copy-done.1, f32[1,384]{1,0:T(1,128)S(1)} %broadcast_in_dim.52.qg_ref, f32[1,384]{1,0:T(1,128)S(1)} %broadcast_in_dim.53.kg_ref, f32[24,1,768]{2,1,0:T(1,128)S(1)} %reshape_reshape.4.bias_ref, bf16[256,768]{1,0:T(8,128)(2,1)S(1)} %copy-done.2), custom_call_target="tpu_custom_call" | custom-call | tf_op jit(solution)/shard_map/pallas_call | solution.py:556
  245.8 0.9 copy.19
  (5 shorter events, 0.0 us)
Async XLA Ops:
  0.0 214.1 %copy-start = (s32[12,2,6]{0,1,2:T(2,128)S(1)}, s32[12,2,6]{0,1,2:T(2,128)}, u32[]{:S(2)}) copy-start(s32[12,2,6]{0,1,2:T(2,128)} %param.25) | copy-start | bytes 1732
  193.3 21.1 %copy-start.2 = (bf16[256,768]{1,0:T(8,128)(2,1)S(1)}, bf16[256,768]{1,0:T(8,128)(2,1)}, u32[]{:S(2)}) copy-start(bf16[256,768]{1,0:T(8,128)(2,1)} %get-tuple-element.10.cache_ref) | copy-start | bytes 1179652
  214.5 2.3 copy-start.1
